TPU v7x, 256 devices: a whole 4x4x8 slice. The times are simulated.
256 devices in a mesh: ctx: 8 (over z), exp: 8 (over y, x_lo), req: 4 (over x_hi, core).
Axes of the slice: x: 4 (x_hi: 2, x_lo: 2; x = x_hi * 2 + x_lo), y: 4, z: 8, core: 2. Of those that a mesh axis runs over, the one named last changes fastest.
Arguments:
- queries: bfloat16 [64, 2, 128, 576], P('req', None, ('ctx', 'exp')), parts along dimension 0, may hold values from -21 to 21
- latent_cache: bfloat16 [64, 32768, 576], P('req', ('ctx', 'exp')), parts along dimension 0, may hold values from -4 to 4
- context_lengths: int32 [64], P('req'), parts along dimension 0, may hold values from 16 to 32767, as said below
- value_up: bfloat16 [128, 512, 128], P(('ctx', 'exp')), may hold values from -0.25 to 0.25
- out_proj: bfloat16 [16384, 7168], P(('ctx', 'exp')), may hold values from -0.09375 to 0.09375
- residual: bfloat16 [128, 7168], P(('req', 'exp')), parts along dimension 0, may hold values from -3 to 3
- norm_gain: bfloat16 [7168], replicated, may hold values from 0.099609375 to 1.8984375
- router: bfloat16 [7168, 8], replicated, may hold values from -0.125 to 0.125
- routes: int32 [128, 2], P(('req', 'exp')), parts along dimension 0, may hold values from 0 to 7, all different within a row; in each aligned block of 4 rows (0 to 3, 4 to 7, ...) at most 2 rows name the same one
- expert_gate: bfloat16 [8, 7168, 1024], P('exp', None, 'ctx'), may hold values from -0.0625 to 0.0625
- expert_up: bfloat16 [8, 7168, 1024], P('exp', None, 'ctx'), may hold values from -0.0625 to 0.0625
- expert_down: bfloat16 [8, 1024, 7168], P('exp', 'ctx'), may hold values from -0.375 to 0.375
Outputs:
- output: bfloat16 [128, 7168], P(('req', 'exp'), 'ctx'), parts along dimension 0
There are 4 independent parts, one for each index of `req`. A program takes and returns all parts, laid end to end along the dimension named above; an argument that names none is the same for every part. Nothing has to cross between parts.
Inputs may be any that keep to these rules, and one draw needn't show every extreme that they name: Verify row j of request r sees context positions below context_lengths[r] + j; in every draw one request has 32767. `routes`: each row names 2 different experts; in each aligned block of 4 rows (the rows of one index of exp) no expert is named by more than 2 rows.
All inputs are finite; a program needn't handle non-finite values.
Results may differ from a plain program's by a relative error of at most 0.028.
Values may be sent and summed in bfloat16 or wider, within the bound.
No kernel may reach another device: no remote copies, remote signals or barrier semaphores. Data moves between devices by JAX's collectives and lax.ppermute only.
A program may use at most 128 MiB of HBM per device.

v0:
```python
import math

import jax
import jax.numpy as jnp
from jax import lax
from jax.sharding import PartitionSpec as P

route_scale = 2.5


def on_device(
    queries,
    latent_cache,
    context_lengths,
    value_up,
    out_proj,
    residual,
    norm_gain,
    router,
    routes,
    expert_gate,
    expert_up,
    expert_down,
):
    latent_width = value_up.shape[1]
    value_width = value_up.shape[2]
    rope_width = queries.shape[3] - latent_width
    score_scale = 1.0 / math.sqrt(value_width + rope_width)
    heads_here = queries.shape[2]
    block_len = latent_cache.shape[1]
    device = lax.axis_index(("ctx", "exp"))
    all_queries = lax.all_gather(queries, ("ctx", "exp"), axis=2, tiled=True)
    scores = (
        jnp.einsum("rjhd,rtd->rjht", all_queries, latent_cache, preferred_element_type=jnp.float32)
        * score_scale
    )
    positions = device * block_len + jnp.arange(block_len, dtype=jnp.int32)
    visible_upto = context_lengths[:, None] + jnp.arange(2, dtype=jnp.int32)[None, :]
    visible = positions[None, None, None, :] < visible_upto[:, :, None, None]
    masked = jnp.where(visible, scores, -1e30)
    row_max = lax.pmax(jnp.max(masked, axis=-1), ("ctx", "exp"))
    weights = jnp.where(visible, jnp.exp(masked - row_max[..., None]), 0.0)
    weight_sum = jnp.sum(weights, axis=-1)
    latents = latent_cache[:, :, :latent_width]
    weighted = jnp.einsum(
        "rjht,rtl->rjhl", weights.astype(jnp.bfloat16), latents, preferred_element_type=jnp.float32
    )
    summed, sum_all = lax.psum((weighted, weight_sum), ("ctx", "exp"))
    own_weighted = lax.dynamic_slice_in_dim(summed, device * heads_here, heads_here, 2)
    own_sum = lax.dynamic_slice_in_dim(sum_all, device * heads_here, heads_here, 2)
    context = (own_weighted / own_sum[..., None]).astype(jnp.bfloat16)
    head_out = jnp.einsum(
        "rjhl,hlv->rjhv", context, value_up, preferred_element_type=jnp.float32
    ).astype(jnp.bfloat16)
    row_total = head_out.shape[0] * head_out.shape[1]
    head_out = head_out.reshape(row_total, heads_here * value_width)
    own_rows = residual.shape[0]
    owner_index = lax.axis_index("exp")
    attention_all = lax.psum(
        jnp.dot(head_out, out_proj, preferred_element_type=jnp.float32), ("ctx", "exp")
    )
    attention = lax.dynamic_slice_in_dim(attention_all, owner_index * own_rows, own_rows, 0)
    hidden = (residual.astype(jnp.float32) + attention).astype(jnp.bfloat16)
    hidden_wide = hidden.astype(jnp.float32)
    inverse = lax.rsqrt(jnp.mean(hidden_wide * hidden_wide, axis=-1, keepdims=True) + 1e-06)
    normed = (hidden_wide * inverse * norm_gain.astype(jnp.float32)).astype(jnp.bfloat16)
    affinity = jax.nn.sigmoid(jnp.dot(normed, router, preferred_element_type=jnp.float32))
    expert_count = router.shape[1]
    top_count = routes.shape[1]
    capacity = max(2, own_rows * top_count // expert_count)
    chosen = (
        routes[:, :, None] == jnp.arange(expert_count, dtype=jnp.int32)[None, None, :]
    ).astype(jnp.float32)
    picked = jnp.sum(chosen * affinity[:, None, :], axis=-1)
    gate_weights = route_scale * picked / jnp.sum(picked, axis=-1, keepdims=True)
    per_row = jnp.sum(chosen, axis=1)
    earlier = jnp.cumsum(per_row, axis=0) - per_row
    slot_index = jnp.sum(chosen * earlier[:, None, :], axis=-1)
    slot_hot = (
        slot_index[:, :, None] == jnp.arange(capacity, dtype=jnp.float32)[None, None, :]
    ).astype(jnp.float32)
    placement = chosen[:, :, :, None] * slot_hot[:, :, None, :]
    row_place = jnp.sum(placement, axis=1).reshape(own_rows, expert_count * capacity)
    gate_place = jnp.sum(placement * gate_weights[:, :, None, None], axis=1).reshape(
        own_rows, expert_count * capacity
    )
    model_width = normed.shape[1]
    outgoing = jnp.einsum(
        "rs,rd->sd", row_place.astype(jnp.bfloat16), normed, preferred_element_type=jnp.float32
    ).astype(jnp.bfloat16)
    outgoing = outgoing.reshape(expert_count, capacity, model_width)
    arrived = lax.all_to_all(outgoing, "exp", split_axis=0, concat_axis=0, tiled=True)
    gate_part = jnp.einsum(
        "scd,df->scf", arrived, expert_gate[0], preferred_element_type=jnp.float32
    )
    up_part = jnp.einsum("scd,df->scf", arrived, expert_up[0], preferred_element_type=jnp.float32)
    active = (jax.nn.silu(gate_part) * up_part).astype(jnp.bfloat16)
    partial_out = jnp.einsum(
        "scf,fd->scd", active, expert_down[0], preferred_element_type=jnp.float32
    )
    col_width = model_width // lax.axis_size("ctx")
    ctx_index = lax.axis_index("ctx")
    own_cols = lax.dynamic_slice_in_dim(hidden_wide, ctx_index * col_width, col_width, 1)
    full_sum = lax.psum(partial_out.astype(jnp.bfloat16), "ctx").astype(jnp.float32)
    returned = lax.all_to_all(
        full_sum.astype(jnp.bfloat16), "exp", split_axis=0, concat_axis=0, tiled=True
    ).astype(full_sum.dtype)
    returned = lax.dynamic_slice_in_dim(returned, ctx_index * col_width, col_width, 2)
    mixture = jnp.dot(
        gate_place,
        returned.reshape(expert_count * capacity, col_width),
        precision=lax.Precision.HIGHEST,
    )
    return (own_cols + mixture).astype(jnp.bfloat16)


def solution(mesh):
    return jax.shard_map(
        on_device,
        mesh=mesh,
        in_specs=(
            P("req", None, ("ctx", "exp"), None),
            P("req", ("ctx", "exp"), None),
            P("req"),
            P(("ctx", "exp"), None, None),
            P(("ctx", "exp"), None),
            P(("req", "exp"), None),
            P(),
            P(),
            P(("req", "exp"), None),
            P("exp", None, "ctx"),
            P("exp", None, "ctx"),
            P("exp", "ctx", None),
        ),
        out_specs=P(("req", "exp"), "ctx"),
        check_vma=False,
    )
```

profile of v0, /device:TPU:4, one launch (start us, length us, event | category | flops | bytes accessed | tf_op | source)
XLA Modules:
  0.0 2005.6 jit_solution(17311653043442676480)
XLA Ops:
  6.5 1.7 copy.38
  8.3 0.7 iota_add_fusion
  9.1 310.2 %all-gather.2.cloned.1.call-done = bf16[16,2,128,576]{3,0,1,2:T(8,128)(2,1)} async-done(((bf16[16,2,2,576]{3,0,1,2:T(8,128)(2,1)}), bf16[16,2,128,576]{3,0,1,2:T(8,128)(2,1)}) %all-gather.2.cloned.1.call-update) | async-done | bytes 4718608 | tf_op jit(solution)/shard_map/all_gather | solution.py:32
  319.4 13.3 fusion.5
  332.7 306.3 %pmax.7 = f32[16,2,128]{2,1,0:T(2,128)S(1)} all-reduce(f32[16,2,128]{2,1,0:T(2,128)S(1)} %get-tuple-element.12), channel_id=1, replica_groups=mesh['ctx'=8,'exp'=8,'req'=4] {'ctx','exp'}, use_global_device_ids=true, to_apply=%region_1.2 | all-reduce | flops 4096 | bytes 32768 | tf_op jit(solution)/shard_map/pmax | solution.py:41
  639.0 11.7 fusion.2
  650.7 11.4 copy.41
  662.3 5.0 fusion.6
  667.2 304.4 %psum.29 = f32[16,2,128]{2,1,0:T(2,128)S(1)} all-reduce(f32[16,2,128]{2,1,0:T(2,128)S(1)} %fusion.6), channel_id=1, replica_groups=mesh['ctx'=8,'exp'=8,'req'=4] {'ctx','exp'}, use_global_device_ids=true, to_apply=%region_4.5 | all-reduce | flops 4096 | bytes 32768 | tf_op jit(solution)/shard_map/psum | solution.py:48
  971.8 328.1 %all-reduce.4.cloned.1.call-done = f32[16,2,128,512]{3,0,2,1:T(8,128)} async-done(((f32[16,2,128,512]{3,0,2,1:T(8,128)}), f32[16,2,128,512]{3,0,2,1:T(8,128)}) %all-reduce.4.cloned.1.call-update) | async-done | bytes 8388624 | tf_op jit(solution)/shard_map/psum | solution.py:48
  1300.0 1.1 fusion.20
  1301.1 3.7 fusion.41
  1305.2 590.4 %all-reduce.6.cloned.1.call-done = f32[32,7168]{1,0:T(8,128)} async-done(((f32[32,7168]{1,0:T(8,128)}), f32[32,7168]{1,0:T(8,128)}) %all-reduce.6.cloned.1.call-update) | async-done | bytes 917520 | tf_op jit(solution)/shard_map/psum | solution.py:59
  1895.6 1.1 multiply_reduce_fusion
  1896.7 0.2 fusion.33
  1897.4 0.3 convolution_convert_fusion
  1897.7 9.6 all_to_all.10
  1907.3 1.9 fusion.18
  1909.2 2.9 convolution_convert_fusion.1
  1912.1 72.3 %all-reduce.8.cloned.1.call-done = bf16[8,2,7168]{2,0,1:T(8,128)(2,1)} async-done(((bf16[8,2,7168]{2,0,1:T(8,128)(2,1)}), bf16[8,2,7168]{2,0,1:T(8,128)(2,1)}) %all-reduce.8.cloned.1.call-update) | async-done | bytes 229392 | tf_op jit(solution)/shard_map/psum | solution.py:104
  1984.4 1.9 copy.48
  1986.3 4.9 all-to-all-start.1
  1991.2 7.1 all-to-all-done.1
  1998.3 0.8 fusion.25
  (38 shorter events, 1.3 us)
Async XLA Ops:
  6.5 1902.6 %copy-start = (bf16[1,128,7168]{2,1,0:T(8,128)(2,1)S(1)}, bf16[1,128,7168]{2,1,0:T(8,128)(2,1)}, u32[]{:S(2)}) copy-start(bf16[1,128,7168]{2,1,0:T(8,128)(2,1)} %param.23) | copy-start | bytes 5505028
  6.5 312.8 %all-gather.2.cloned.1.call-start = ((), (), s32[]{:S(2)}) async-start(), calls=%async_computation.2 | async-start | bytes 5324800 | tf_op jit(solution)/shard_map/all_gather | solution.py:32
  8.2 1291.7 %all-reduce.4.cloned.1.call-start = ((), (), s32[]{:S(2)}) async-start(), calls=%async_computation.3 | async-start | bytes 16777216 | tf_op jit(solution)/shard_map/psum | solution.py:48
  662.1 637.8 %copy-start.4 = (bf16[2,512,128]{2,1,0:T(8,128)(2,1)S(1)}, bf16[2,512,128]{2,1,0:T(8,128)(2,1)}, u32[]{:S(2)}) copy-start(bf16[2,512,128]{2,1,0:T(8,128)(2,1)} %param.15) | copy-start | bytes 786436
  662.2 642.8 %copy-start.2 = (bf16[7168]{0:T(1024)(128)(2,1)S(1)}, bf16[7168]{0:T(1024)(128)(2,1)}, u32[]{:S(2)}) copy-start(bf16[7168]{0:T(1024)(128)(2,1)} %param.18) | copy-start | bytes 43012
  662.2 642.8 %copy-start.3 = (s32[4,2]{0,1:T(2,128)S(1)}, s32[4,2]{0,1:T(2,128)}, u32[]{:S(2)}) copy-start(s32[4,2]{0,1:T(2,128)} %param.20) | copy-start | bytes 100
  662.2 1233.4 %copy-start.1 = (bf16[4,7168]{1,0:T(4,128)(2,1)S(1)}, bf16[4,7168]{1,0:T(4,128)(2,1)}, u32[]{:S(2)}) copy-start(bf16[4,7168]{1,0:T(4,128)(2,1)} %param.17) | copy-start | bytes 172036
  662.2 1234.5 %copy-start.5 = (bf16[7168,8]{0,1:T(8,128)(2,1)S(1)}, bf16[7168,8]{0,1:T(8,128)(2,1)}, u32[]{:S(2)}) copy-start(bf16[7168,8]{0,1:T(8,128)(2,1)} %param.19) | copy-start | bytes 344068
  662.2 1233.3 %all-reduce.6.cloned.1.call-start = ((), (), s32[]{:S(2)}) async-start(), calls=%async_computation.4 | async-start | bytes 1835008 | tf_op jit(solution)/shard_map/psum | solution.py:59
  1304.9 679.5 %all-reduce.8.cloned.1.call-start = ((), (), s32[]{:S(2)}) async-start(), calls=%async_computation.5 | async-start | bytes 458752 | tf_op jit(solution)/shard_map/psum | solution.py:104
  1986.3 12.0 all-to-all-start.1
Sparse Core Ops, SparseCore 0:
  9.1 310.1 all-gather.1
  662.3 637.6 all-reduce.3
  1305.0 590.5 all-reduce.5
  1912.2 72.1 all-reduce.7
where the time goes:
time: 2010 us
  waiting for transfers between devices  1310 us (65%)
  blocking collectives  620 us (31%)
  matrix products  35.9 us (2%)
    psum x1, waiting for transfers between devices, on_device(): lax.psum(jnp.dot(head_out, out_proj, preferred_element_type=jnp.float32),...  590 us
    psum x1, waiting for transfers between devices, on_device(): summed, sum_all = lax.psum((weighted, weight_sum), ('ctx', 'exp'))  328 us
    all_gather x1, waiting for transfers between devices, on_device(): all_queries = lax.all_gather(queries, ('ctx', 'exp'), axis=2, tiled=True)  310 us
    pmax x1, blocking collectives, on_device(): row_max = lax.pmax(jnp.max(masked, axis=-1), ('ctx', 'exp'))  306 us
    psum x1, blocking collectives, on_device(): summed, sum_all = lax.psum((weighted, weight_sum), ('ctx', 'exp'))  304 us
    psum x1, waiting for transfers between devices, on_device(): lax.psum(partial_out.astype(jnp.bfloat16), 'ctx').astype(jnp.float32)  72.3 us
  transfers between devices with their start and end apart: 5, of which 5 were waited for; matrix products, arithmetic and copies ran while one was open for 0% of the time, Pallas kernels for 0%

commit v1 on v0

v1 whole, which is shorter than its diff:
```python
import functools
import math

import jax
import jax.numpy as jnp
from jax import lax
from jax.experimental import pallas as pl
from jax.experimental.pallas import tpu as pltpu
from jax.sharding import PartitionSpec as P

route_scale = 2.5
f32 = jnp.float32
bf16 = jnp.bfloat16
VMEM_LIMIT = 48 * 1024 * 1024


def iota(shape, dim):
    return lax.broadcasted_iota(jnp.int32, shape, dim)


def dot(a, b, dims=((1,), (0,))):
    return lax.dot_general(a, b, (dims, ((), ())), preferred_element_type=f32)


def attend_kernel(scale, n_ctx, n_exp, lengths, base, q_ref, k_ref, routes_ref, out_ref, perm_ref, stat_ref):
    step = pl.program_id(0)
    requests = pl.num_programs(0) - 1
    per = q_ref.shape[2]
    rows = n_ctx * per
    width = out_ref.shape[2]
    per_pair = rows // (n_ctx * n_exp)
    chunk = out_ref.shape[1]

    @pl.when(step == 0)
    def _():
        to, frm = iota((rows, rows), 0), iota((rows, rows), 1)
        group = n_ctx * per_pair
        e, c, rest = to // group, (to % group) // per_pair, to % per_pair
        perm_ref[...] = (frm == c * per + e * per_pair + rest).astype(bf16)
        stat_ref[...] = jnp.zeros_like(stat_ref)

    @pl.when(step < requests)
    def _():
        q = dot(perm_ref[...], q_ref[...].reshape(rows, q_ref.shape[3])).astype(bf16)
        k = k_ref[0]
        scores = dot(q, k, ((1,), (1,))) * scale
        block = k.shape[0]
        row = iota((rows, 1), 0)
        limit = lengths[step] + (row // 2) % 2 - base[0]
        visible = iota((rows, block), 1) < limit
        masked = jnp.where(visible, scores, -1e30)
        top = jnp.max(masked, axis=1, keepdims=True).astype(bf16).astype(f32)
        weights = jnp.where(visible, jnp.exp(masked - top), 0.0)
        total = jnp.sum(weights, axis=1, keepdims=True)
        got = dot(weights.astype(bf16), k[:, :width])
        out_ref[...] = got.astype(bf16).reshape(n_exp, chunk, width)
        here = (iota((chunk, width), 1) == step * chunk + iota((chunk, width), 0))[None]
        stat_ref[0] += jnp.sum(jnp.where(here, top.reshape(n_exp, chunk, 1), 0.0), axis=1)
        stat_ref[1] += jnp.sum(jnp.where(here, total.reshape(n_exp, chunk, 1), 0.0), axis=1)

    @pl.when(step == requests)
    def _():
        top, total = stat_ref[0], stat_ref[1]
        high = total.astype(bf16).astype(f32)
        row = iota((n_exp, chunk, width), 1)
        table = jnp.where(row == 0, top[:, None, :], 0.0)
        table = jnp.where(row == 1, high[:, None, :], table)
        table = jnp.where(row == 2, (total - high)[:, None, :], table)
        table = jnp.where(row == 3, routes_ref[...][None], table)
        out_ref[...] = table.astype(bf16)


def attend(queries, cache, lengths, base, routes_row, scale, n_exp, lat):
    n_ctx, reqs, per, depth = queries.shape
    block = cache.shape[1]
    rows = n_ctx * per
    chunk = rows // n_exp
    last = reqs - 1
    return pl.pallas_call(
        functools.partial(attend_kernel, scale, n_ctx, n_exp),
        out_shape=jax.ShapeDtypeStruct((n_exp, (reqs + 1) * chunk, lat), bf16),
        grid_spec=pltpu.PrefetchScalarGridSpec(
            num_scalar_prefetch=2,
            grid=(reqs + 1,),
            in_specs=[
                pl.BlockSpec((n_ctx, 1, per, depth), lambda r, *_: (0, jnp.minimum(r, last), 0, 0)),
                pl.BlockSpec((1, block, depth), lambda r, *_: (jnp.minimum(r, last), 0, 0)),
                pl.BlockSpec((1, lat), lambda r, *_: (0, 0)),
            ],
            out_specs=pl.BlockSpec((n_exp, chunk, lat), lambda r, *_: (0, r, 0)),
            scratch_shapes=[pltpu.VMEM((rows, rows), bf16), pltpu.VMEM((2, n_exp, lat), f32)],
        ),
        compiler_params=pltpu.CompilerParams(vmem_limit_bytes=VMEM_LIMIT),
        name="attend",
    )(lengths, base, queries, cache, routes_row)


def merge_kernel(n_ctx, in_ref, out_ref, sum_ref):
    sources, _, width = in_ref.shape
    rows = sum_ref.shape[0]
    chunk = in_ref.shape[1] - rows
    reqs = rows // chunk
    part = chunk // n_ctx
    own = reqs * part
    table = in_ref[:, rows : rows + 16, :].astype(f32)
    tops = table[:, 0, :]
    sums = table[:, 1, :] + table[:, 2, :]
    top = jnp.max(tops, axis=0, keepdims=True)
    factor = jnp.exp(tops - top)
    total = jnp.sum(factor * sums, axis=0, keepdims=True)
    columns = factor.T
    for r in range(reqs):
        lo = r * chunk
        acc = jnp.zeros((chunk, width), f32)
        for s in range(sources):
            acc += in_ref[s, lo : lo + chunk, :].astype(f32) * columns[lo : lo + chunk, s : s + 1]
        sum_ref[lo : lo + chunk, :] = acc.astype(bf16)
    to, frm = iota((rows, rows), 0), iota((rows, rows), 1)
    c, r, rest = to // own, (to % own) // part, to % part
    perm = (frm == r * chunk + c * part + rest).astype(bf16)
    out_ref[:, :own, :] = dot(perm, sum_ref[...]).astype(bf16).reshape(n_ctx, own, width)
    high = total.astype(bf16).astype(f32)
    row = iota((16, rows), 0)
    packed = jnp.where(row == 0, top, 0.0)
    packed = jnp.where(row == 1, high, packed)
    packed = jnp.where(row == 2, total - high, packed)
    moved = dot(packed.astype(bf16), perm, ((1,), (1,))).astype(bf16)
    out_ref[:, own : own + 16, :] = jnp.broadcast_to(moved[None], (n_ctx, 16, rows))


def merge(arrived, n_ctx, reqs):
    n_exp, tall, lat = arrived.shape
    chunk = tall // (reqs + 1)
    rows = reqs * chunk
    own = rows // n_ctx
    return pl.pallas_call(
        functools.partial(merge_kernel, n_ctx),
        out_shape=jax.ShapeDtypeStruct((n_ctx, own + 16, lat), bf16),
        scratch_shapes=[pltpu.VMEM((rows, lat), bf16)],
        compiler_params=pltpu.CompilerParams(vmem_limit_bytes=VMEM_LIMIT),
        name="merge",
    )(arrived)


def project_kernel(place, in_ref, up_ref, proj_ref, out_ref, head_ref):
    sources, tall, lat = in_ref.shape
    own = tall - 16
    heads, _, vdim = up_ref.shape

    @pl.when(pl.program_id(0) == 0)
    def _():
        mine = (iota((own, lat), 1) == place[0] * own + iota((own, lat), 0)).astype(bf16)
        table = in_ref[:, own : own + 16, :]
        tops = dot(mine, table[:, 0, :], ((1,), (1,)))
        sums = dot(mine, table[:, 1, :], ((1,), (1,))) + dot(mine, table[:, 2, :], ((1,), (1,)))
        factor = jnp.exp(tops - jnp.max(tops, axis=1, keepdims=True))
        total = jnp.sum(factor * sums, axis=1, keepdims=True)
        acc = jnp.zeros((own, lat), f32)
        for s in range(sources):
            acc += in_ref[s, :own, :].astype(f32) * factor[:, s : s + 1]
        context = (acc / total).astype(bf16)
        for h in range(heads):
            value = dot(context, up_ref[h]).astype(bf16)
            pick = (iota((own // heads, own), 1) == heads * iota((own // heads, own), 0) + h).astype(bf16)
            head_ref[:, h * vdim : (h + 1) * vdim] = dot(pick, value).astype(bf16)

    out_ref[0] = dot(head_ref[...], proj_ref[...]).astype(bf16)


def project(arrived, place, value_up, out_proj, n_ctx):
    sources, tall, lat = arrived.shape
    heads, _, vdim = value_up.shape
    model = out_proj.shape[1]
    cols = model // n_ctx
    rows = (tall - 16) // heads
    return pl.pallas_call(
        project_kernel,
        out_shape=jax.ShapeDtypeStruct((n_ctx, rows, cols), bf16),
        grid_spec=pltpu.PrefetchScalarGridSpec(
            num_scalar_prefetch=1,
            grid=(n_ctx,),
            in_specs=[
                pl.BlockSpec((sources, tall, lat), lambda c, *_: (0, 0, 0)),
                pl.BlockSpec((heads, lat, vdim), lambda c, *_: (0, 0, 0)),
                pl.BlockSpec((heads * vdim, cols), lambda c, *_: (0, c)),
            ],
            out_specs=pl.BlockSpec((1, rows, cols), lambda c, *_: (c, 0, 0)),
            scratch_shapes=[pltpu.VMEM((rows, heads * vdim), bf16)],
        ),
        compiler_params=pltpu.CompilerParams(vmem_limit_bytes=VMEM_LIMIT),
        name="project",
    )(place, arrived, value_up, out_proj)


def expert_kernel(me, hid_ref, gain_ref, router_ref, routes_ref, gate_ref, up_ref, down_ref, out_ref):
    blocks, rows, cols = hid_ref.shape
    experts = router_ref.shape[1]
    square = jnp.zeros((rows, 1), f32)
    for c in range(blocks):
        h = hid_ref[c].astype(f32)
        square += jnp.sum(h * h, axis=1, keepdims=True)
    inverse = lax.rsqrt(square / (blocks * cols) + 1e-06)
    gate = jnp.zeros((rows, gate_ref.shape[2]), f32)
    up = jnp.zeros((rows, up_ref.shape[2]), f32)
    logits = jnp.zeros((rows, experts), f32)
    for c in range(blocks):
        normed = (hid_ref[c].astype(f32) * inverse * gain_ref[c].astype(f32)).astype(bf16)
        gate += dot(normed, gate_ref[c])
        up += dot(normed, up_ref[c])
        logits += dot(normed, router_ref[c], ((1,), (1,)))
    affinity = jax.nn.sigmoid(logits)
    lane = iota((rows, experts), 1)
    mine = jnp.zeros((rows, 1), f32)
    whole = jnp.zeros((rows, 1), f32)
    for k in range(routes_ref.shape[1]):
        choice = routes_ref[:, k : k + 1]
        picked = jnp.sum(jnp.where(lane == choice, affinity, 0.0), axis=1, keepdims=True)
        whole += picked
        mine += jnp.where(choice == me[0], picked, 0.0)
    weight = route_scale * mine / whole
    active = (gate / (1.0 + jnp.exp(-gate)) * up).astype(bf16)
    for c in range(blocks):
        got = dot(active, down_ref[:, c * cols : (c + 1) * cols])
        out_ref[c] = (got * weight).astype(bf16)


def experts_here(hidden, gain, router, routes, me, gate, up, down):
    vmem = pl.BlockSpec(memory_space=pltpu.VMEM)
    return pl.pallas_call(
        expert_kernel,
        out_shape=jax.ShapeDtypeStruct(hidden.shape, bf16),
        in_specs=[pl.BlockSpec(memory_space=pltpu.SMEM)] + [vmem] * 7,
        out_specs=vmem,
        compiler_params=pltpu.CompilerParams(vmem_limit_bytes=VMEM_LIMIT),
        name="experts",
    )(me, hidden, gain, router, routes, gate, up, down)


def on_device(
    queries,
    latent_cache,
    context_lengths,
    value_up,
    out_proj,
    residual,
    norm_gain,
    router,
    routes,
    expert_gate,
    expert_up,
    expert_down,
):
    reqs, pair, heads, depth = queries.shape
    lat, vdim = value_up.shape[1:]
    scale = 1.0 / math.sqrt(vdim + depth - lat)
    n_ctx, n_exp = lax.axis_size("ctx"), lax.axis_size("exp")
    n_all = n_ctx * n_exp
    everyone = ("ctx", "exp")
    ctx, exp = lax.axis_index("ctx"), lax.axis_index("exp")
    own_rows, model = residual.shape
    top = routes.shape[1]
    cols = model // n_ctx
    experts = router.shape[1]

    def swap(x, axes):
        return lax.all_to_all(x, axes, split_axis=0, concat_axis=0, tiled=True)

    q = queries.reshape(reqs * pair * heads, depth)
    q = swap(jnp.broadcast_to(q[None], (n_exp, *q.shape)), "exp")
    q = q.reshape(n_exp, reqs, pair * heads, depth).transpose(1, 0, 2, 3)
    q = lax.all_gather(q.reshape(reqs, n_exp * pair * heads, depth), "ctx", axis=0)

    base = ((ctx * n_exp + exp) * latent_cache.shape[1]).reshape(1)
    routes_row = jnp.zeros((1, lat), f32).at[0, : own_rows * top].set(routes.reshape(-1).astype(f32))
    sent = attend(q, latent_cache, context_lengths, base, routes_row, scale, n_exp, lat)
    arrived = swap(sent, "exp")
    table_row = arrived.shape[1] // (reqs + 1) * reqs + 3
    all_routes = arrived[:, table_row, : own_rows * top].astype(jnp.int32).reshape(n_exp * own_rows, top)
    arrived = swap(merge(arrived, n_ctx, reqs), "ctx")
    terms = project(arrived, ctx.reshape(1), value_up, out_proj, n_ctx)

    terms = swap(terms.reshape(n_all, own_rows, cols), everyone)
    attention = jnp.sum(terms.astype(f32), axis=0)
    own = lax.dynamic_slice_in_dim(residual, ctx * cols, cols, 1)
    hidden = (own.astype(f32) + attention).astype(bf16)
    rows = swap(jnp.broadcast_to(hidden[None], (n_all, own_rows, cols)), everyone)
    mixed = experts_here(
        rows.reshape(n_ctx, n_exp * own_rows, cols),
        norm_gain.reshape(n_ctx, 1, cols),
        router.T.reshape(experts, n_ctx, cols).transpose(1, 0, 2),
        all_routes,
        exp.reshape(1),
        expert_gate.reshape(n_ctx, cols, -1),
        expert_up.reshape(n_ctx, cols, -1),
        expert_down[0],
    )
    mixed = swap(mixed.reshape(n_all, own_rows, cols), everyone)
    mixture = jnp.sum(mixed.astype(f32), axis=0)
    return (hidden.astype(f32) + mixture).astype(bf16)


def solution(mesh):
    return jax.shard_map(
        on_device,
        mesh=mesh,
        in_specs=(
            P("req", None, ("ctx", "exp"), None),
            P("req", ("ctx", "exp"), None),
            P("req"),
            P(("ctx", "exp"), None, None),
            P(("ctx", "exp"), None),
            P(("req", "exp"), None),
            P(),
            P(),
            P(("req", "exp"), None),
            P("exp", None, "ctx"),
            P("exp", None, "ctx"),
            P("exp", "ctx", None),
        ),
        out_specs=P(("req", "exp"), "ctx"),
        check_vma=False,
    )
```

time: 2010 us -> 270 us (0.13)
  waiting for transfers between devices: 1310 us -> 77.9 us
  blocking collectives: 620 us -> 115 us
  matrix products: 35.9 us -> 0 us
  Pallas kernels: 0 us -> 26.5 us
    psum x3 -> x0, waiting for transfers between devices: 991 us -> none  [the longest x1 590 us: on_device(): lax.psum(jnp.dot(head_out, out_proj, preferred_element_type=jnp.float32),...]
    pmax x1 -> x0, blocking collectives: 306 us -> none  [on_device(): row_max = lax.pmax(jnp.max(masked, axis=-1), ('ctx', 'exp'))]
    psum x1 -> x0, blocking collectives: 304 us -> none  [on_device(): summed, sum_all = lax.psum((weighted, weight_sum), ('ctx', 'exp'))]
    all_gather x1, waiting for transfers between devices: 310 us -> 50 us  [on_device(): lax.all_gather(q.reshape(reqs, n_exp * pair * heads, depth), 'ctx', axis=0)]
    all_to_all x1 -> x4, blocking collectives: 9.57 us -> 115 us  [swap(): return lax.all_to_all(x, axes, split_axis=0, concat_axis=0, tiled=True)]
    dot_general x9 -> x0, matrix products: 35.9 us -> none  [the longest x1 13.3 us: on_device(): jnp.einsum('rjhd,rtd->rjht', all_queries, latent_cache, preferred_element...]
    pallas_call x0 -> x4, Pallas kernels: none -> 26.5 us  [the longest x1 19.1 us: attend(): pl.pallas_call(functools.partial(attend_kernel, scale, n_ctx, n_exp), out...]
    all_to_all x1 -> x2, waiting for transfers between devices: 7.11 us -> 27.8 us  [swap(): return lax.all_to_all(x, axes, split_axis=0, concat_axis=0, tiled=True)]
  transfers between devices with their start and end apart: 5 -> 3, of which waited for: 5 -> 3; matrix products, arithmetic and copies ran while one was open for 0% -> 6% of each run, Pallas kernels for 0% -> 0%
where the time goes in v1:
time: 270 us; the launch traced here: 269 us
  blocking collectives  115 us (43%)
  waiting for transfers between devices  77.9 us (29%)
  Pallas kernels  26.5 us (10%)
  local copies, waits for them, and re-layouts  22.6 us (8%)
  between operations  13.6 us (5%)
  starting transfers between devices  9.51 us (4%)
  other arithmetic  3.81 us (1%)
    all_to_all x4, blocking collectives, swap(): return lax.all_to_all(x, axes, split_axis=0, concat_axis=0, tiled=True)  115 us
    all_gather x1, waiting for transfers between devices, on_device(): lax.all_gather(q.reshape(reqs, n_exp * pair * heads, depth), 'ctx', axis=0)  50 us
    all_to_all x2, waiting for transfers between devices, swap(): return lax.all_to_all(x, axes, split_axis=0, concat_axis=0, tiled=True)  27.8 us
    pallas_call x1, Pallas kernels, attend(): pl.pallas_call(functools.partial(attend_kernel, scale, n_ctx, n_exp), out...  19.1 us
    unnamed x19, local copies, waits for them, and re-layouts  17.7 us
    all_to_all x2, starting transfers between devices, swap(): return lax.all_to_all(x, axes, split_axis=0, concat_axis=0, tiled=True)  9.51 us
  transfers between devices with their start and end apart: 3, of which 3 were waited for; matrix products, arithmetic and copies ran while one was open for 6% of the time, Pallas kernels for 0%

profile of v1, /device:TPU:4, one launch (start us, length us, event | category | flops | bytes accessed | tf_op | source)
XLA Modules:
  0.0 268.6 jit_solution(9730857138651175917)
XLA Ops:
  6.5 1.0 broadcast_in_dim.6
  7.6 16.5 %all_to_all.30 = bf16[8,64,576]{2,1,0:T(8,128)(2,1)S(1)} all-to-all(bf16[8,64,576]{2,1,0:T(8,128)(2,1)S(1)} %broadcast_in_dim.7), channel_id=1, replica_groups=mesh['ctx'=8,'exp'=8,'req'=4] {'exp'}, dimensions={0} | all-to-all | bytes 1179648 | tf_op jit(solution)/shard_map/all_to_all | solution.py:266
  24.6 1.0 copy.25
  25.7 14.1 %copy.27.k_ref = bf16[16,512,576]{2,1,0:T(8,128)(2,1)} copy(bf16[16,512,576]{1,2,0:T(8,128)(2,1)} %param.15) | data formatting | bytes 18874368 | tf_op args[1]
  39.9 0.7 compare_reduce_fusion
  40.6 0.6 convert_select_fusion
  41.4 50.0 %all-gather.2.cloned.1.call-done.q_ref = bf16[8,16,32,576]{3,2,1,0:T(8,128)(2,1)} async-done(((bf16[1,16,32,576]{3,2,1,0:T(8,128)(2,1)}), bf16[8,16,32,576]{3,2,1,0:T(8,128)(2,1)}) %all-gather.2.cloned.1.call-update) | async-done | bytes 4718608 | tf_op jit(solution)/shard_map/all_gather | solution.py:271
  91.4 19.1 %attend.1 = bf16[8,544,512]{2,1,0:T(8,128)(2,1)S(1)} custom-call(s32[16]{0:T(128)S(1)} %copy-done.6, s32[1]{0:T(128)} %bitcast.1.base, bf16[8,16,32,576]{3,2,1,0:T(8,128)(2,1)} %all-gather.2.cloned.1.call-done.q_ref, bf16[16,512,576]{2,1,0:T(8,128)(2,1)} %copy.27.k_ref, f32[1,512]{1,0:T(1,128)S(1)} %scatter.4.routes_ref), custom_call_target="tpu_custom_call" | custom-call | tf_op jit(solution)/shard_map/attend/pallas_call | solution.py:79
  110.6 57.6 %all_to_all.31.in_ref = bf16[8,544,512]{2,1,0:T(8,128)(2,1)S(1)} all-to-all(bf16[8,544,512]{2,1,0:T(8,128)(2,1)S(1)} %attend.1), channel_id=1, replica_groups=mesh['ctx'=8,'exp'=8,'req'=4] {'exp'}, dimensions={0} | all-to-all | bytes 8912896 | tf_op jit(solution)/shard_map/all_to_all | solution.py:266
  168.2 1.6 merge.1
  169.8 2.0 copy-done
  171.8 23.2 %all_to_all.32.in_ref = bf16[8,80,512]{2,1,0:T(8,128)(2,1)S(1)} all-to-all(bf16[8,80,512]{2,1,0:T(8,128)(2,1)S(1)} %merge.1), channel_id=1, replica_groups=mesh['ctx'=8,'exp'=8,'req'=4] {'ctx'}, dimensions={0} | all-to-all | bytes 1310720 | tf_op jit(solution)/shard_map/all_to_all | solution.py:266
  195.1 3.0 %project.1 = bf16[8,32,896]{2,1,0:T(8,128)(2,1)S(1)} custom-call(s32[1]{0:T(128)} %bitcast.place, bf16[8,80,512]{2,1,0:T(8,128)(2,1)S(1)} %all_to_all.32.in_ref, bf16[2,512,128]{2,1,0:T(8,128)(2,1)S(1)} %copy-done.4, bf16[256,7168]{1,0:T(8,128)(2,1)S(1)} %copy-done.1), custom_call_target="tpu_custom_call" | custom-call | tf_op jit(solution)/shard_map/project/pallas_call | solution.py:176
  198.0 0.9 reshape.87
  198.9 4.6 %all-to-all-start.3 = ((bf16[64,4,896]{2,1,0:T(4,128)(2,1)}), bf16[64,4,896]{2,1,0:T(4,128)(2,1)S(1)}, u32[]{:S(2)}, u32[]{:S(2)}) async-start(bf16[64,4,896]{2,1,0:T(4,128)(2,1)} %reshape.87), calls=%async_computation.3 | async-start | bytes 917504 | tf_op jit(solution)/shard_map/all_to_all | solution.py:266
  203.6 14.3 %all-to-all-done.3 = bf16[64,4,896]{2,1,0:T(4,128)(2,1)S(1)} async-done(((bf16[64,4,896]{2,1,0:T(4,128)(2,1)}), bf16[64,4,896]{2,1,0:T(4,128)(2,1)S(1)}, u32[]{:S(2)}, u32[]{:S(2)}) %all-to-all-start.3) | async-done | bytes 458784 | tf_op jit(solution)/shard_map/all_to_all | solution.py:266
  218.1 0.7 add_convert_fusion.1
  218.8 0.9 broadcast_in_dim.16
  219.7 4.9 %all-to-all-start.4 = ((bf16[64,4,896]{2,1,0:T(4,128)(2,1)}), bf16[64,4,896]{2,1,0:T(4,128)(2,1)S(1)}, u32[]{:S(2)}, u32[]{:S(2)}) async-start(bf16[64,4,896]{2,1,0:T(4,128)(2,1)} %broadcast_in_dim.16), calls=%async_computation.4 | async-start | bytes 917504 | tf_op jit(solution)/shard_map/all_to_all | solution.py:266
  224.6 0.7 fusion
  225.4 13.5 %all-to-all-done.4 = bf16[64,4,896]{2,1,0:T(4,128)(2,1)S(1)} async-done(((bf16[64,4,896]{2,1,0:T(4,128)(2,1)}), bf16[64,4,896]{2,1,0:T(4,128)(2,1)S(1)}, u32[]{:S(2)}, u32[]{:S(2)}) %all-to-all-start.4) | async-done | bytes 458784 | tf_op jit(solution)/shard_map/all_to_all | solution.py:266
  239.1 1.5 copy-done.3
  240.6 2.9 %experts.1 = bf16[8,32,896]{2,1,0:T(8,128)(2,1)S(1)} custom-call(s32[1]{0:T(128)} %bitcast.5.me, bf16[8,32,896]{2,1,0:T(8,128)(2,1)S(1)} %reshape.89.hid_ref, bf16[8,1,896]{2,1,0:T(2,128)(2,1)S(1)} %reshape.96.gain_ref, bf16[8,8,896]{2,1,0:T(8,128)(2,1)S(1)} %bitcast.17, s32[32,2]{1,0:T(8,128)S(1)} %reshape.95.routes_ref, bf16[8,896,128]{2,1,0:T(8,128)(2,1)S(1)} %bitcast.15, ...), custom_call_target="tpu_custom_call" | custom-call | tf_op jit(solution)/shard_map/experts/pallas_call | solution.py:229
  243.6 17.3 %all_to_all.33 = bf16[64,4,896]{2,1,0:T(4,128)(2,1)S(1)} all-to-all(bf16[64,4,896]{2,1,0:T(4,128)(2,1)S(1)} %reshape.94), channel_id=1, replica_groups=mesh['ctx'=8,'exp'=8,'req'=4] {'ctx','exp'}, dimensions={0} | all-to-all | bytes 917504 | tf_op jit(solution)/shard_map/all_to_all | solution.py:266
  (31 shorter events, 2.2 us)
Async XLA Ops:
  6.5 84.9 %all-gather.2.cloned.1.call-start = ((), (), s32[]{:S(2)}) async-start(), calls=%async_computation.6 | async-start | bytes 5898240 | tf_op jit(solution)/shard_map/all_gather | solution.py:271
  25.7 14.9 %copy-start.8 = (s32[4,2]{0,1:T(2,128)S(1)}, s32[4,2]{0,1:T(2,128)}, u32[]{:S(2)}) copy-start(s32[4,2]{0,1:T(2,128)} %param.22) | copy-start | bytes 100
  25.7 65.7 %copy-start.6 = (s32[16]{0:T(128)S(1)}, s32[16]{0:T(128)}, u32[]{:S(2)}) copy-start(s32[16]{0:T(128)} %lengths.1) | copy-start | bytes 196
  168.2 26.8 %copy-start.1 = (bf16[256,7168]{1,0:T(8,128)(2,1)S(1)}, bf16[256,7168]{1,0:T(8,128)(2,1)}, u32[]{:S(2)}) copy-start(bf16[256,7168]{1,0:T(8,128)(2,1)} %proj_ref.1) | copy-start | bytes 11010052
  168.2 26.8 %copy-start.4 = (bf16[2,512,128]{2,1,0:T(8,128)(2,1)S(1)}, bf16[2,512,128]{2,1,0:T(8,128)(2,1)}, u32[]{:S(2)}) copy-start(bf16[2,512,128]{2,1,0:T(8,128)(2,1)} %up_ref.1) | copy-start | bytes 786436
  169.8 2.0 copy-start
  195.0 29.5 %copy-start.7 = (bf16[7168]{0:T(1024)(128)(2,1)S(1)}, bf16[7168]{0:T(1024)(128)(2,1)}, u32[]{:S(2)}) copy-start(bf16[7168]{0:T(1024)(128)(2,1)} %param.20) | copy-start | bytes 43012
  195.0 44.0 %copy-start.2 = (bf16[1,7168,128]{2,1,0:T(8,128)(2,1)S(1)}, bf16[1,7168,128]{2,1,0:T(8,128)(2,1)}, u32[]{:S(2)}) copy-start(bf16[1,7168,128]{2,1,0:T(8,128)(2,1)} %param.23) | copy-start | bytes 5505028
  195.0 44.0 %copy-start.5 = (bf16[7168,8]{0,1:T(8,128)(2,1)S(1)}, bf16[7168,8]{0,1:T(8,128)(2,1)}, u32[]{:S(2)}) copy-start(bf16[7168,8]{0,1:T(8,128)(2,1)} %param.21) | copy-start | bytes 344068
  198.9 18.9 %all-to-all-start.3 = ((bf16[64,4,896]{2,1,0:T(4,128)(2,1)}), bf16[64,4,896]{2,1,0:T(4,128)(2,1)S(1)}, u32[]{:S(2)}, u32[]{:S(2)}) async-start(bf16[64,4,896]{2,1,0:T(4,128)(2,1)} %reshape.87), calls=%async_computation.3 | async-start | bytes 917504 | tf_op jit(solution)/shard_map/all_to_all | solution.py:266
  219.7 19.3 %all-to-all-start.4 = ((bf16[64,4,896]{2,1,0:T(4,128)(2,1)}), bf16[64,4,896]{2,1,0:T(4,128)(2,1)S(1)}, u32[]{:S(2)}, u32[]{:S(2)}) async-start(bf16[64,4,896]{2,1,0:T(4,128)(2,1)} %broadcast_in_dim.16), calls=%async_computation.4 | async-start | bytes 917504 | tf_op jit(solution)/shard_map/all_to_all | solution.py:266
  239.1 1.5 copy-start.3
Sparse Core Ops, SparseCore 0:
  25.8 65.5 all-gather.1

commit v2 on v1

v2 whole, which is shorter than its diff:
```python
import functools
import math

import jax
import jax.numpy as jnp
from jax import lax
from jax.experimental import pallas as pl
from jax.experimental.pallas import tpu as pltpu
from jax.sharding import PartitionSpec as P

route_scale = 2.5
f32 = jnp.float32
bf16 = jnp.bfloat16
VMEM_LIMIT = 16 * 1024 * 1024
LANES = 128
LOG2E = math.log2(math.e)
TABLE = 16


def iota(shape, dim):
    return lax.broadcasted_iota(jnp.int32, shape, dim)


def dot(a, b, dims=((1,), (0,))):
    return lax.dot_general(a, b, (dims, ((), ())), preferred_element_type=f32)


def in_hbm(x):
    return pltpu.with_memory_space_constraint(x, pltpu.HBM)


def attend_kernel(scale, n_ctx, n_exp, first, permuted, lengths, base, q_ref, k_ref, routes_ref, out_ref, *scratch):
    stat_ref, buf_ref, table_ref, sems = scratch[:4]
    step = pl.program_id(0)
    slot = lax.rem(step, 2)
    n_outer, unroll, per, depth = q_ref.shape
    rows = n_outer * per
    chunk = rows // n_exp
    block = k_ref.shape[2]
    tall = out_ref.shape[1] - TABLE
    lines = stat_ref.shape[2] // LANES
    tiles = tall // (unroll * pl.num_programs(0) * chunk)
    width = tiles * LANES

    @pl.when(step == 0)
    def _():
        stat_ref[...] = jnp.zeros_like(stat_ref)
        if permuted:
            per_pair = rows // (n_ctx * n_exp)
            to, frm = iota((rows, rows), 0), iota((rows, rows), 1)
            e, c, rest = to // chunk, (to % chunk) // per_pair, to % per_pair
            scratch[4][...] = (frm == c * per + e * per_pair + rest).astype(bf16)

    row = iota((rows, 1), 0)
    lane = iota((rows, block), 1)
    span = buf_ref.shape[2]

    def leave(which, where):
        place = out_ref.at[:, pl.ds(pl.multiple_of(where * span, span), span), :]
        return pltpu.make_async_copy(buf_ref.at[which], place, sems.at[which])

    @pl.when(step >= 2)
    def _():
        leave(slot, step - 2).wait()

    for u in range(unroll):
        r = step * unroll + u
        q = q_ref[:, u].reshape(rows, depth)
        if permuted:
            q = dot(scratch[4][...], q).astype(bf16)
        k = k_ref[u]
        scores = dot(q, k) * (scale * LOG2E)
        visible = lane < lengths[first + r] + (row // 2) % 2 - base[0]
        masked = jnp.where(visible, scores, -1e30)
        top = jnp.maximum(jnp.max(masked, axis=1, keepdims=True), -1e29).astype(bf16).astype(f32)
        weights = jnp.exp2(masked - top)
        total = jnp.sum(weights, axis=1, keepdims=True)
        got = dot(weights.astype(bf16), k[:width], ((1,), (1,)))
        got = got.astype(bf16).reshape(n_exp, chunk, width)
        for t in range(tiles):
            lo = (u * tiles + t) * chunk
            buf_ref[slot, :, lo : lo + chunk, :] = got[:, :, t * LANES : (t + 1) * LANES]
        spot = iota((chunk, lines * LANES), 1) == r * chunk + iota((chunk, lines * LANES), 0)
        spot = spot[None]
        stat_ref[0] += jnp.sum(jnp.where(spot, top.reshape(n_exp, chunk, 1), 0.0), axis=1)
        stat_ref[1] += jnp.sum(jnp.where(spot, total.reshape(n_exp, chunk, 1), 0.0), axis=1)

    leave(slot, step).start()

    @pl.when(step == pl.num_programs(0) - 1)
    def _():
        top, total = stat_ref[0], stat_ref[1]
        high = total.astype(bf16).astype(f32)
        line = iota((n_exp, TABLE, LANES), 1)
        table = jnp.where(line == TABLE - 1, routes_ref[...][None], 0.0)
        for kind, values in enumerate((top, high, total - high)):
            for w in range(lines):
                part = values[:, w * LANES : (w + 1) * LANES]
                table = jnp.where(line == kind * lines + w, part[:, None, :], table)
        table_ref[...] = table.astype(bf16)
        last = pltpu.make_async_copy(table_ref, out_ref.at[:, pl.ds(tall, TABLE), :], sems.at[2])
        last.start()

        @pl.when(step >= 1)
        def _():
            leave(1 - slot, step - 1).wait()

        leave(slot, step).wait()
        last.wait()


def attend(queries, cache, lengths, base, routes_row, scale, n_ctx, n_exp, lat, first, permuted):
    n_outer, reqs, per, depth = queries.shape
    block = cache.shape[2]
    rows = n_outer * per
    unroll = 2 if reqs % 2 == 0 and first % 2 == 0 else 1
    chunk = rows // n_exp
    tall = reqs * chunk * (lat // LANES) + TABLE
    wide = -(-reqs * chunk // LANES) * LANES
    return pl.pallas_call(
        functools.partial(attend_kernel, scale, n_ctx, n_exp, first, permuted),
        out_shape=pltpu.HBM((n_exp, tall, LANES), bf16),
        grid_spec=pltpu.PrefetchScalarGridSpec(
            num_scalar_prefetch=2,
            grid=(reqs // unroll,),
            in_specs=[
                pl.BlockSpec((n_outer, unroll, per, depth), lambda r, *_: (0, r, 0, 0)),
                pl.BlockSpec((unroll, depth, block), lambda r, *_: (r + first // unroll, 0, 0)),
                pl.BlockSpec((1, LANES), lambda r, *_: (0, 0)),
            ],
            out_specs=pl.BlockSpec(memory_space=pltpu.HBM),
            scratch_shapes=[
                pltpu.VMEM((2, n_exp, wide), f32),
                pltpu.VMEM((2, n_exp, unroll * chunk * (lat // LANES), LANES), bf16),
                pltpu.VMEM((n_exp, TABLE, LANES), bf16),
                pltpu.SemaphoreType.DMA((3,)),
            ]
            + ([pltpu.VMEM((rows, rows), bf16)] if permuted else []),
        ),
        compiler_params=pltpu.CompilerParams(vmem_limit_bytes=VMEM_LIMIT),
        cost_estimate=pl.CostEstimate(
            flops=4 * reqs * rows * block * depth,
            bytes_accessed=2 * reqs * (depth * block + rows * (depth + lat)),
            transcendentals=reqs * rows * block,
        ),
        name="attend",
    )(lengths, base, queries, cache, routes_row)


def merge_rows(in_ref, sum_ref, first, count):
    sources, tall, _ = in_ref.shape
    tall -= TABLE
    tiles = sum_ref.shape[1] // LANES
    chunk = tall // (count * tiles)
    lines = -(-count * chunk // LANES)
    table = in_ref[:, tall : tall + TABLE, :].astype(f32)

    def kind(n):
        return jnp.concatenate([table[:, n * lines + w, :] for w in range(lines)], axis=1)

    tops, sums = kind(0), kind(1) + kind(2)
    top = jnp.max(tops, axis=0, keepdims=True)
    factor = jnp.exp2(tops - top)
    columns = factor.T
    for r in range(count):
        lo = r * chunk
        for t in range(tiles):
            acc = jnp.zeros((chunk, LANES), f32)
            for s in range(sources):
                at = (r * tiles + t) * chunk
                acc += in_ref[s, at : at + chunk, :].astype(f32) * columns[lo : lo + chunk, s : s + 1]
            sum_ref[first + lo : first + lo + chunk, t * LANES : (t + 1) * LANES] = acc.astype(bf16)
    total = jnp.sum(factor * sums, axis=0, keepdims=True)
    return top[:, : count * chunk], total[:, : count * chunk], table[:, TABLE - 1, :]


def merge_early_kernel(count, in_ref, sum_ref, stat_ref, routes_ref):
    top, total, routes_ref[...] = merge_rows(in_ref, sum_ref, 0, count)
    line = iota(stat_ref.shape, 0)
    stat_ref[...] = jnp.where(line == 0, top, jnp.where(line == 1, total, 0.0))


def merge_early(arrived, count, lat):
    sources, tall, _ = arrived.shape
    rows = (tall - TABLE) // (lat // LANES)
    return pl.pallas_call(
        functools.partial(merge_early_kernel, count),
        out_shape=(
            jax.ShapeDtypeStruct((rows, lat), bf16),
            jax.ShapeDtypeStruct((8, rows), f32),
            jax.ShapeDtypeStruct((sources, LANES), f32),
        ),
        compiler_params=pltpu.CompilerParams(vmem_limit_bytes=VMEM_LIMIT),
        cost_estimate=pl.CostEstimate(
            flops=4 * arrived.size, bytes_accessed=2 * arrived.size, transcendentals=sources * rows
        ),
        name="merge_early",
    )(arrived)


def merge_late_kernel(n_ctx, count, early_ref, stat_ref, in_ref, far_ref, out_ref, sum_ref, up_ref, sem):
    rows, lat = sum_ref.shape
    first = early_ref.shape[0]
    fetch = pltpu.make_async_copy(far_ref, up_ref, sem)
    fetch.start()
    heads = up_ref.shape[1]
    reqs = count * rows // (rows - first)
    sum_ref[:first, :] = early_ref[...]
    top, total, _ = merge_rows(in_ref, sum_ref, first, count)
    top = jnp.concatenate([stat_ref[0:1, :], top], axis=1)
    total = jnp.concatenate([stat_ref[1:2, :], total], axis=1)
    own = rows // n_ctx
    part = own // reqs
    pairs = own // heads
    pair = part // heads
    to, frm = iota((rows, rows), 0), iota((rows, rows), 1)
    c, h, r, j = to // own, (to % own) // pairs, (to % pairs) // pair, to % pair
    perm = (frm == r * n_ctx * part + c * part + j * heads + h).astype(bf16)
    moved = dot(perm, sum_ref[...]).astype(bf16)
    fetch.wait()
    for c in range(n_ctx):
        for h in range(heads):
            lo = c * own + h * pairs
            value = dot(moved[lo : lo + pairs], up_ref[c, h])
            out_ref[c, h * pairs : (h + 1) * pairs, :] = value.astype(bf16)
    high = total.astype(bf16).astype(f32)
    line = iota((TABLE, rows), 0)
    packed = jnp.where(line == 0, top, 0.0)
    packed = jnp.where(line == 1, high, packed)
    packed = jnp.where(line == 2, total - high, packed)
    table = dot(packed.astype(bf16), perm, ((1,), (1,))).astype(bf16)
    for c in range(n_ctx):
        lo = c * own // LANES * LANES
        out_ref[c, own : own + TABLE, :] = table[:, lo : lo + LANES]


def merge_late(early, stats, arrived, value_up, count):
    n_ctx, heads, lat, vdim = value_up.shape
    rows = early.shape[0] + (arrived.shape[1] - TABLE) // (lat // LANES)
    return pl.pallas_call(
        functools.partial(merge_late_kernel, n_ctx, count),
        out_shape=jax.ShapeDtypeStruct((n_ctx, rows // n_ctx + TABLE, vdim), bf16),
        in_specs=[pl.BlockSpec(memory_space=pltpu.VMEM)] * 3 + [pl.BlockSpec(memory_space=pltpu.HBM)],
        scratch_shapes=[
            pltpu.VMEM((rows, lat), bf16),
            pltpu.VMEM((n_ctx, heads, lat, vdim), bf16),
            pltpu.SemaphoreType.DMA,
        ],
        compiler_params=pltpu.CompilerParams(vmem_limit_bytes=VMEM_LIMIT),
        name="merge_late",
    )(early, stats, arrived, in_hbm(value_up))


def project_kernel(place, in_ref, far_ref, out_ref, proj_ref, sum_ref, sems):
    sources, tall, vdim = in_ref.shape
    own = tall - TABLE
    blocks, rows, cols = out_ref.shape
    heads = own // rows
    copies = []
    for h in range(heads):
        part = pl.ds(h * vdim, vdim)
        copies.append(pltpu.make_async_copy(far_ref.at[part], proj_ref.at[part], sems.at[h]))
        copies[h].start()
    offset = lax.rem(place[0] * own, LANES)
    mine = (iota((own, LANES), 1) == offset + iota((own, LANES), 0)).astype(bf16)
    table = in_ref[:, own : own + TABLE, :]
    tops = dot(mine, table[:, 0, :], ((1,), (1,)))
    sums = dot(mine, table[:, 1, :], ((1,), (1,))) + dot(mine, table[:, 2, :], ((1,), (1,)))
    factor = jnp.exp2(tops - jnp.max(tops, axis=1, keepdims=True))
    total = jnp.sum(factor * sums, axis=1, keepdims=True)
    acc = jnp.zeros((own, vdim), f32)
    for s in range(sources):
        acc += in_ref[s, :own, :].astype(f32) * factor[:, s : s + 1]
    value = (acc / total).astype(bf16)
    for h in range(heads):
        copies[h].wait()
        for c in range(blocks):
            weight = proj_ref[h * vdim : (h + 1) * vdim, c * cols : (c + 1) * cols]
            term = dot(value[h * rows : (h + 1) * rows], weight)
            if h > 0:
                term += sum_ref[c]
            if h < heads - 1:
                sum_ref[c] = term
            else:
                out_ref[c] = term.astype(bf16)


def project(arrived, place, out_proj, n_ctx):
    sources, tall, vdim = arrived.shape
    depth, model = out_proj.shape
    cols = model // n_ctx
    rows = (tall - TABLE) * vdim // depth
    vmem = pl.BlockSpec(memory_space=pltpu.VMEM)
    return pl.pallas_call(
        project_kernel,
        out_shape=jax.ShapeDtypeStruct((n_ctx, rows, cols), bf16),
        in_specs=[pl.BlockSpec(memory_space=pltpu.SMEM), vmem, pl.BlockSpec(memory_space=pltpu.HBM)],
        out_specs=vmem,
        scratch_shapes=[
            pltpu.VMEM(out_proj.shape, bf16),
            pltpu.VMEM((n_ctx, rows, cols), f32),
            pltpu.SemaphoreType.DMA((depth // vdim,)),
        ],
        compiler_params=pltpu.CompilerParams(vmem_limit_bytes=VMEM_LIMIT),
        name="project",
    )(place, arrived, in_hbm(out_proj))


def expert_kernel(me, hid_ref, gain_ref, router_ref, routes_ref, gate_ref, *refs):
    far_refs, out_ref, (up_ref, down_ref, normed_ref, sems) = refs[:2], refs[2], refs[3:]
    blocks, rows, cols = hid_ref.shape
    experts = router_ref.shape[1]
    half_up, half_down = blocks // 2, down_ref.shape[0] // 2
    pieces = [(0, pl.ds(0, half_up)), (0, pl.ds(half_up, blocks - half_up))]
    pieces += [(1, pl.ds(0, half_down)), (1, pl.ds(half_down, half_down))]
    copies = [
        pltpu.make_async_copy(far_refs[n].at[piece], (up_ref, down_ref)[n].at[piece], sems.at[i])
        for i, (n, piece) in enumerate(pieces)
    ]
    for copy in copies:
        copy.start()
    square = jnp.zeros((rows, 1), f32)
    for c in range(blocks):
        h = hid_ref[c].astype(f32)
        square += jnp.sum(h * h, axis=1, keepdims=True)
    inverse = lax.rsqrt(square / (blocks * cols) + 1e-06)
    gate = jnp.zeros((rows, gate_ref.shape[2]), f32)
    up = jnp.zeros((rows, up_ref.shape[2]), f32)
    logits = jnp.zeros((rows, experts), f32)
    for c in range(blocks):
        normed = (hid_ref[c].astype(f32) * inverse * gain_ref[c].astype(f32)).astype(bf16)
        gate += dot(normed, gate_ref[c])
        logits += dot(normed, router_ref[c], ((1,), (1,)))
        normed_ref[c] = normed
    for c in range(blocks):
        if c == 0 or c == half_up:
            copies[c // half_up].wait()
        up += dot(normed_ref[c], up_ref[c])
    affinity = jax.nn.sigmoid(logits)
    lane = iota((rows, experts), 1)
    mine = jnp.zeros((rows, 1), f32)
    whole = jnp.zeros((rows, 1), f32)
    for k in range(routes_ref.shape[1]):
        choice = routes_ref[:, k : k + 1]
        picked = jnp.sum(jnp.where(lane == choice, affinity, 0.0), axis=1, keepdims=True)
        whole += picked
        mine += jnp.where(choice == me[0], picked, 0.0)
    weight = route_scale * mine / whole
    copies[2].wait()
    copies[3].wait()
    active = (gate / (1.0 + jnp.exp(-gate)) * up).astype(bf16)
    for c in range(blocks):
        got = dot(active, down_ref[:, c * cols : (c + 1) * cols])
        out_ref[c] = (got * weight).astype(bf16)


def experts_here(hidden, gain, router, routes, me, gate, up, down):
    vmem = pl.BlockSpec(memory_space=pltpu.VMEM)
    return pl.pallas_call(
        expert_kernel,
        out_shape=jax.ShapeDtypeStruct(hidden.shape, bf16),
        in_specs=[pl.BlockSpec(memory_space=pltpu.SMEM)]
        + [vmem] * 5
        + [pl.BlockSpec(memory_space=pltpu.HBM)] * 2,
        out_specs=vmem,
        scratch_shapes=[
            pltpu.VMEM(up.shape, bf16),
            pltpu.VMEM(down.shape, bf16),
            pltpu.VMEM(hidden.shape, bf16),
            pltpu.SemaphoreType.DMA((4,)),
        ],
        compiler_params=pltpu.CompilerParams(vmem_limit_bytes=VMEM_LIMIT),
        name="experts",
    )(me, hidden, gain, router, routes, gate, in_hbm(up), in_hbm(down))


def on_device(
    queries,
    latent_cache,
    context_lengths,
    value_up,
    out_proj,
    residual,
    norm_gain,
    router,
    routes,
    expert_gate,
    expert_up,
    expert_down,
):
    reqs, pair, heads, depth = queries.shape
    lat, vdim = value_up.shape[1:]
    scale = 1.0 / math.sqrt(vdim + depth - lat)
    n_ctx, n_exp = lax.axis_size("ctx"), lax.axis_size("exp")
    n_all = n_ctx * n_exp
    everyone = ("ctx", "exp")
    ctx, exp = lax.axis_index("ctx"), lax.axis_index("exp")
    own_rows, model = residual.shape
    top = routes.shape[1]
    cols = model // n_ctx
    experts = router.shape[1]

    def swap(x, axes):
        return lax.all_to_all(x, axes, split_axis=0, concat_axis=0, tiled=True)

    def spread(x, axes, size):
        return swap(jnp.broadcast_to(x[None], (size, *x.shape)), axes)

    early = reqs * 5 // 16
    counts = (early, reqs - early)
    per = pair * heads
    q = queries.reshape(reqs * per, depth)
    late = spread(q[early * per :], "exp", n_exp)
    late = late.reshape(n_exp, counts[1], per, depth).transpose(1, 0, 2, 3).reshape(counts[1], n_exp * per, depth)
    q, late = lax.optimization_barrier((q[: early * per], late))
    late = lax.all_gather(late, "ctx", axis=0)
    q = spread(q, "ctx", n_ctx)
    q = q.reshape(n_ctx, early, per, depth).transpose(1, 0, 2, 3).reshape(early * n_ctx * per, depth)
    q = spread(q, "exp", n_exp).reshape(n_exp, early, n_ctx * per, depth)

    base = ((ctx * n_exp + exp) * latent_cache.shape[1]).reshape(1)
    routes_row = jnp.zeros((1, LANES), f32).at[0, : own_rows * top].set(routes.reshape(-1).astype(f32))
    cache = in_hbm(latent_cache.swapaxes(1, 2))
    rest = (cache, context_lengths, base, routes_row, scale, n_ctx, n_exp, lat)
    sent = attend(q, *rest, 0, False)
    up, late = lax.optimization_barrier((value_up, late))
    all_up = lax.all_gather(up, "ctx", axis=0)
    late = in_hbm(late)
    arrived = swap(sent, "exp")
    sent, arrived = lax.optimization_barrier((attend(late, *rest, early, True), arrived))
    sums, stats, route_rows = merge_early(arrived, early, lat)
    all_routes = route_rows[:, : own_rows * top].astype(jnp.int32).reshape(n_exp, own_rows, top)
    sent, sums = lax.optimization_barrier((sent, sums))
    arrived = swap(sent, "exp")
    arrived = swap(merge_late(sums, stats, arrived, all_up, reqs - early), "ctx")
    terms = project(arrived, ctx.reshape(1), out_proj, n_ctx)

    terms = swap(terms.reshape(n_all, own_rows, cols), everyone)
    attention = jnp.sum(terms.astype(f32), axis=0)
    own = lax.dynamic_slice_in_dim(residual, ctx * cols, cols, 1)
    hidden = (own.astype(f32) + attention).astype(bf16)

    slots = max(2, own_rows * top // experts)
    before = jnp.tril(jnp.ones((own_rows, own_rows), jnp.int32), -1)

    def slot_of(named, axis):
        shape = (1,) * axis + (own_rows, own_rows) + (1,) * (named.ndim - 1 - axis)
        earlier = jnp.sum(before.reshape(shape) * jnp.expand_dims(named, axis), axis=axis + 1)
        return jnp.where(named == 1, earlier, -1)

    named = jnp.sum((routes[:, :, None] == jnp.arange(experts)).astype(jnp.int32), axis=1)
    place = (slot_of(named, 0)[:, :, None] == jnp.arange(slots)).astype(bf16)
    place = jnp.broadcast_to(place[:, None], (own_rows, n_ctx, experts, slots)).reshape(own_rows, -1)
    rows = dot(place, hidden, ((0,), (0,))).astype(bf16)
    rows = swap(rows.reshape(n_all, slots, cols), everyone)

    named = jnp.any(all_routes == exp, axis=2).astype(jnp.int32)
    taken = (slot_of(named, 1)[:, None, :] == jnp.arange(slots)[None, :, None]).astype(jnp.int32)
    slot_routes = jnp.sum(taken[..., None] * all_routes[:, None], axis=2).reshape(n_exp * slots, top)
    mixed = experts_here(
        rows.reshape(n_ctx, n_exp * slots, cols),
        norm_gain.reshape(n_ctx, 1, cols),
        router.T.reshape(experts, n_ctx, cols).transpose(1, 0, 2),
        slot_routes,
        exp.reshape(1),
        expert_gate.reshape(n_ctx, cols, -1),
        expert_up.reshape(n_ctx, cols, -1),
        expert_down[0],
    )
    mixed = swap(mixed.reshape(n_all, slots, cols), everyone)
    mixture = dot(place, mixed.reshape(n_all * slots, cols))
    return (hidden.astype(f32) + mixture).astype(bf16)


def solution(mesh):
    return jax.shard_map(
        on_device,
        mesh=mesh,
        in_specs=(
            P("req", None, ("ctx", "exp"), None),
            P("req", ("ctx", "exp"), None),
            P("req"),
            P(("ctx", "exp"), None, None),
            P(("ctx", "exp"), None),
            P(("req", "exp"), None),
            P(),
            P(),
            P(("req", "exp"), None),
            P("exp", None, "ctx"),
            P("exp", None, "ctx"),
            P("exp", "ctx", None),
        ),
        out_specs=P(("req", "exp"), "ctx"),
        check_vma=False,
    )
```

time: 270 us -> 219 us (0.81)
  blocking collectives: 115 us -> 34.4 us
  waiting for transfers between devices: 77.9 us -> 99.8 us
  starting transfers between devices: 9.51 us -> 29.9 us
  local copies, waits for them, and re-layouts: 22.6 us -> 7.01 us
  Pallas kernels: 26.5 us -> 29.7 us
    all_to_all x4 -> x2, blocking collectives: 115 us -> 34.4 us  [swap(): return lax.all_to_all(x, axes, split_axis=0, concat_axis=0, tiled=True)]
    all_to_all x2 -> x7, waiting for transfers between devices: 27.8 us -> 99.1 us  [swap(): return lax.all_to_all(x, axes, split_axis=0, concat_axis=0, tiled=True)]
    all_gather x1 -> x2, waiting for transfers between devices: 50 us -> 0.02 us  [the longest x1 0.02 us: on_device(): late = lax.all_gather(late, 'ctx', axis=0)]
    all_to_all x2 -> x7, starting transfers between devices: 9.51 us -> 29.9 us  [swap(): return lax.all_to_all(x, axes, split_axis=0, concat_axis=0, tiled=True)]
    unnamed x19 -> x10, local copies, waits for them, and re-layouts: 17.7 us -> 0.02 us
    pallas_call x2 -> x4, Pallas kernels: 20.7 us -> 24.2 us  [the longest x2 21 us: attend(): pl.pallas_call(functools.partial(attend_kernel, scale, n_ctx, n_exp, firs...]
  transfers between devices with their start and end apart: 3 -> 9, of which waited for: 3 -> 7; matrix products, arithmetic and copies ran while one was open for 6% -> 2% of each run, Pallas kernels for 0% -> 10%
where the time goes in v2:
time: 219 us; the launch traced here: 218 us
  waiting for transfers between devices  99.8 us (46%)
  blocking collectives  34.4 us (16%)
  starting transfers between devices  29.9 us (14%)
  Pallas kernels  29.7 us (14%)
  between operations  13.7 us (6%)
  local copies, waits for them, and re-layouts  7.01 us (3%)
  other arithmetic  2.67 us (1%)
    all_to_all x7, waiting for transfers between devices, swap(): return lax.all_to_all(x, axes, split_axis=0, concat_axis=0, tiled=True)  99.1 us
    all_to_all x2, blocking collectives, swap(): return lax.all_to_all(x, axes, split_axis=0, concat_axis=0, tiled=True)  34.4 us
    all_to_all x7, starting transfers between devices, swap(): return lax.all_to_all(x, axes, split_axis=0, concat_axis=0, tiled=True)  29.9 us
    pallas_call x2, Pallas kernels, attend(): pl.pallas_call(functools.partial(attend_kernel, scale, n_ctx, n_exp, firs...  21 us
  transfers between devices with their start and end apart: 9, of which 7 were waited for; matrix products, arithmetic and copies ran while one was open for 2% of the time, Pallas kernels for 10%

profile of v2, /device:TPU:4, one launch (start us, length us, event | category | flops | bytes accessed | tf_op | source)
XLA Modules:
  0.0 218.3 jit_solution(9970209521086709533)
XLA Ops:
  8.3 5.1 %all-to-all-start = ((bf16[8,44,576]{2,1,0:T(8,128)(2,1)}), bf16[8,44,576]{2,1,0:T(8,128)(2,1)S(1)}, u32[]{:S(2)}, u32[]{:S(2)}) async-start(bf16[8,44,576]{2,1,0:T(8,128)(2,1)} %broadcast_in_dim.20), calls=%async_computation | async-start | bytes 983040 | tf_op jit(solution)/shard_map/all_to_all | solution.py:404
  13.5 9.6 %all-to-all-done = bf16[8,44,576]{2,1,0:T(8,128)(2,1)S(1)} async-done(((bf16[8,44,576]{2,1,0:T(8,128)(2,1)}), bf16[8,44,576]{2,1,0:T(8,128)(2,1)S(1)}, u32[]{:S(2)}, u32[]{:S(2)}) %all-to-all-start) | async-done | bytes 405536 | tf_op jit(solution)/shard_map/all_to_all | solution.py:404
  23.4 1.0 reshape.171
  24.5 18.7 %all_to_all.45 = bf16[8,20,576]{2,1,0:T(8,128)(2,1)S(1)} all-to-all(bf16[8,20,576]{2,1,0:T(8,128)(2,1)S(1)} %broadcast_in_dim.21), channel_id=1, replica_groups=mesh['ctx'=8,'exp'=8,'req'=4] {'ctx'}, dimensions={0} | all-to-all | bytes 368640 | tf_op jit(solution)/shard_map/all_to_all | solution.py:404
  43.4 1.3 broadcast_in_dim.23
  44.7 3.7 %all-to-all-start.2 = ((bf16[8,160,576]{2,1,0:T(8,128)(2,1)}), bf16[8,160,576]{2,1,0:T(8,128)(2,1)S(1)}, u32[]{:S(2)}, u32[]{:S(2)}) async-start(bf16[8,160,576]{2,1,0:T(8,128)(2,1)} %broadcast_in_dim.23), calls=%async_computation.2 | async-start | bytes 3276800 | tf_op jit(solution)/shard_map/all_to_all | solution.py:404
  50.0 18.2 %all-to-all-done.2 = bf16[8,160,576]{2,1,0:T(8,128)(2,1)S(1)} async-done(((bf16[8,160,576]{2,1,0:T(8,128)(2,1)}), bf16[8,160,576]{2,1,0:T(8,128)(2,1)S(1)}, u32[]{:S(2)}, u32[]{:S(2)}) %all-to-all-start.2) | async-done | bytes 1474592 | tf_op jit(solution)/shard_map/all_to_all | solution.py:404
  68.1 6.9 %attend.3 = bf16[8,656,128]{2,1,0:T(8,128)(2,1)} custom-call(s32[16]{0:T(128)S(1)} %copy-done.2, s32[1]{0:T(128)} %bitcast.1.base, bf16[8,5,32,576]{3,2,1,0:T(8,128)(2,1)S(1)} %bitcast.28, bf16[16,576,512]{2,1,0:T(8,128)(2,1)} %bitcast.32, f32[1,128]{1,0:T(1,128)S(1)} %scatter.4.routes_ref), custom_call_target="tpu_custom_call" | custom-call | flops 1509949440 | bytes 5734400 | tf_op jit(solution)/shard_map/attend/pallas_call | solution.py:120
  75.0 3.6 %all-to-all-start.3 = ((bf16[8,656,128]{2,1,0:T(8,128)(2,1)}), bf16[8,656,128]{2,1,0:T(8,128)(2,1)S(1)}, u32[]{:S(2)}, u32[]{:S(2)}) async-start(bf16[8,656,128]{2,1,0:T(8,128)(2,1)} %attend.3), calls=%async_computation.3 | async-start | bytes 2686976 | tf_op jit(solution)/shard_map/all_to_all | solution.py:404
  79.3 14.1 %attend.2 = bf16[8,1424,128]{2,1,0:T(8,128)(2,1)} custom-call(s32[16]{0:T(128)S(1)} %copy-done.2, s32[1]{0:T(128)} %bitcast.1.base, bf16[8,11,32,576]{3,2,1,0:T(8,128)(2,1)} %bitcast.34, bf16[16,576,512]{2,1,0:T(8,128)(2,1)} %bitcast.33, f32[1,128]{1,0:T(1,128)S(1)} %scatter.4.routes_ref), custom_call_target="tpu_custom_call" | custom-call | flops 3321888768 | bytes 12615680 | tf_op jit(solution)/shard_map/attend/pallas_call | solution.py:120
  93.5 1.8 all-to-all-done.3.in_ref
  95.7 3.8 %all-to-all-start.4 = ((bf16[8,1424,128]{2,1,0:T(8,128)(2,1)}), bf16[8,1424,128]{2,1,0:T(8,128)(2,1)S(1)}, u32[]{:S(2)}, u32[]{:S(2)}) async-start(bf16[8,1424,128]{2,1,0:T(8,128)(2,1)} %attend.2), calls=%async_computation.4 | async-start | bytes 5832704 | tf_op jit(solution)/shard_map/all_to_all | solution.py:404
  99.6 33.0 %all-to-all-done.4.in_ref = bf16[8,1424,128]{2,1,0:T(8,128)(2,1)S(1)} async-done(((bf16[8,1424,128]{2,1,0:T(8,128)(2,1)}), bf16[8,1424,128]{2,1,0:T(8,128)(2,1)S(1)}, u32[]{:S(2)}, u32[]{:S(2)}) %all-to-all-start.4) | async-done | bytes 2916384 | tf_op jit(solution)/shard_map/all_to_all | solution.py:404
  132.6 2.8 %merge_late.1 = bf16[8,80,128]{2,1,0:T(8,128)(2,1)} custom-call(bf16[160,512]{1,0:T(8,128)(2,1)S(1)} %get-tuple-element.34.early_ref, f32[8,160]{1,0:T(8,128)S(1)} %get-tuple-element.35.stat_ref, bf16[8,1424,128]{2,1,0:T(8,128)(2,1)S(1)} %all-to-all-done.4.in_ref, bf16[8,2,512,128]{3,2,1,0:T(8,128)(2,1)} %bitcast.35), custom_call_target="tpu_custom_call" | custom-call | tf_op jit(solution)/shard_map/merge_late/pallas_call | solution.py:240
  135.4 3.4 %all-to-all-start.5 = ((bf16[8,80,128]{2,1,0:T(8,128)(2,1)}), bf16[8,80,128]{2,1,0:T(8,128)(2,1)S(1)}, u32[]{:S(2)}, u32[]{:S(2)}) async-start(bf16[8,80,128]{2,1,0:T(8,128)(2,1)} %merge_late.1), calls=%async_computation.5 | async-start | bytes 327680 | tf_op jit(solution)/shard_map/all_to_all | solution.py:404
  138.9 9.3 %all-to-all-done.5.in_ref = bf16[8,80,128]{2,1,0:T(8,128)(2,1)S(1)} async-done(((bf16[8,80,128]{2,1,0:T(8,128)(2,1)}), bf16[8,80,128]{2,1,0:T(8,128)(2,1)S(1)}, u32[]{:S(2)}, u32[]{:S(2)}) %all-to-all-start.5) | async-done | bytes 163872 | tf_op jit(solution)/shard_map/all_to_all | solution.py:404
  148.1 2.5 %project.1 = bf16[8,32,896]{2,1,0:T(8,128)(2,1)S(1)} custom-call(s32[1]{0:T(128)} %bitcast.place, bf16[8,80,128]{2,1,0:T(8,128)(2,1)S(1)} %all-to-all-done.5.in_ref, bf16[256,7168]{1,0:T(8,128)(2,1)} %far_ref.1), custom_call_target="tpu_custom_call" | custom-call | tf_op jit(solution)/shard_map/project/pallas_call | solution.py:294
  150.6 0.9 reshape.175
  151.5 4.8 %all-to-all-start.6 = ((bf16[64,4,896]{2,1,0:T(4,128)(2,1)}), bf16[64,4,896]{2,1,0:T(4,128)(2,1)S(1)}, u32[]{:S(2)}, u32[]{:S(2)}) async-start(bf16[64,4,896]{2,1,0:T(4,128)(2,1)} %reshape.175), calls=%async_computation.6 | async-start | bytes 917504 | tf_op jit(solution)/shard_map/all_to_all | solution.py:404
  156.7 15.7 %all-to-all-done.6 = bf16[64,4,896]{2,1,0:T(4,128)(2,1)S(1)} async-done(((bf16[64,4,896]{2,1,0:T(4,128)(2,1)}), bf16[64,4,896]{2,1,0:T(4,128)(2,1)S(1)}, u32[]{:S(2)}, u32[]{:S(2)}) %all-to-all-start.6) | async-done | bytes 458784 | tf_op jit(solution)/shard_map/all_to_all | solution.py:404
  174.3 5.5 %all-to-all-start.7 = ((bf16[64,2,896]{2,1,0:T(2,128)(2,1)}), bf16[64,2,896]{2,1,0:T(2,128)(2,1)S(1)}, u32[]{:S(2)}, u32[]{:S(2)}) async-start(bf16[64,2,896]{2,1,0:T(2,128)(2,1)} %reshape.178), calls=%async_computation.7 | async-start | bytes 458752 | tf_op jit(solution)/shard_map/all_to_all | solution.py:404
  180.0 11.6 %all-to-all-done.7 = bf16[64,2,896]{2,1,0:T(2,128)(2,1)S(1)} async-done(((bf16[64,2,896]{2,1,0:T(2,128)(2,1)}), bf16[64,2,896]{2,1,0:T(2,128)(2,1)S(1)}, u32[]{:S(2)}, u32[]{:S(2)}) %all-to-all-start.7) | async-done | bytes 229408 | tf_op jit(solution)/shard_map/all_to_all | solution.py:404
  191.7 3.0 %experts.1 = bf16[8,16,896]{2,1,0:T(8,128)(2,1)S(1)} custom-call(s32[1]{0:T(128)} %bitcast.11.me, bf16[8,16,896]{2,1,0:T(8,128)(2,1)S(1)} %reshape.179.hid_ref, bf16[8,1,896]{2,1,0:T(2,128)(2,1)S(1)} %reshape.190.gain_ref, bf16[8,8,896]{2,1,0:T(8,128)(2,1)S(1)} %bitcast.30, s32[16,2]{1,0:T(8,128)S(1)} %bitcast.31, bf16[8,896,128]{2,1,0:T(8,128)(2,1)S(1)} %bitcast.29, ...), custom_call_target="tpu_custom_call" | custom-call | tf_op jit(solution)/shard_map/experts/pallas_call | solution.py:359
  194.8 15.8 %all_to_all.46 = bf16[64,2,896]{2,1,0:T(2,128)(2,1)S(1)} all-to-all(bf16[64,2,896]{2,1,0:T(2,128)(2,1)S(1)} %reshape.186), channel_id=1, replica_groups=mesh['ctx'=8,'exp'=8,'req'=4] {'ctx','exp'}, dimensions={0} | all-to-all | bytes 458752 | tf_op jit(solution)/shard_map/all_to_all | solution.py:404
  (61 shorter events, 8.7 us)
Async XLA Ops:
  6.5 6.9 %slice-start = ((bf16[16,2,2,576]{3,2,1,0:T(2,128)(2,1)}), bf16[5,2,2,576]{3,2,1,0:T(2,128)(2,1)S(1)}, s32[]{:S(2)}) async-start(bf16[16,2,2,576]{3,2,1,0:T(2,128)(2,1)} %param.14), calls=%async_computation.11 | async-start | bytes 51200 | tf_op jit(solution)/shard_map/slice | solution.py:415
  8.3 14.8 %all-to-all-start = ((bf16[8,44,576]{2,1,0:T(8,128)(2,1)}), bf16[8,44,576]{2,1,0:T(8,128)(2,1)S(1)}, u32[]{:S(2)}, u32[]{:S(2)}) async-start(bf16[8,44,576]{2,1,0:T(8,128)(2,1)} %broadcast_in_dim.20), calls=%async_computation | async-start | bytes 983040 | tf_op jit(solution)/shard_map/all_to_all | solution.py:404
  13.4 65.2 %all-gather.5.cloned.1.call-start = ((), (), s32[]{:S(2)}) async-start(), calls=%async_computation.9 | async-start | bytes 4055040 | tf_op jit(solution)/shard_map/all_gather | solution.py:416
  44.7 4.4 %copy-start.4 = (s32[4,2]{0,1:T(2,128)S(1)}, s32[4,2]{0,1:T(2,128)}, u32[]{:S(2)}) copy-start(s32[4,2]{0,1:T(2,128)} %param.22) | copy-start | bytes 100
  44.7 23.4 %copy-start.2 = (s32[16]{0:T(128)S(1)}, s32[16]{0:T(128)}, u32[]{:S(2)}) copy-start(s32[16]{0:T(128)} %lengths.3) | copy-start | bytes 196
  44.7 23.4 %all-to-all-start.2 = ((bf16[8,160,576]{2,1,0:T(8,128)(2,1)}), bf16[8,160,576]{2,1,0:T(8,128)(2,1)S(1)}, u32[]{:S(2)}, u32[]{:S(2)}) async-start(bf16[8,160,576]{2,1,0:T(8,128)(2,1)} %broadcast_in_dim.23), calls=%async_computation.2 | async-start | bytes 3276800 | tf_op jit(solution)/shard_map/all_to_all | solution.py:404
  75.0 20.3 %all-to-all-start.3 = ((bf16[8,656,128]{2,1,0:T(8,128)(2,1)}), bf16[8,656,128]{2,1,0:T(8,128)(2,1)S(1)}, u32[]{:S(2)}, u32[]{:S(2)}) async-start(bf16[8,656,128]{2,1,0:T(8,128)(2,1)} %attend.3), calls=%async_computation.3 | async-start | bytes 2686976 | tf_op jit(solution)/shard_map/all_to_all | solution.py:404
  78.6 54.0 %all-gather.7.cloned.1.call-start = ((), (), s32[]{:S(2)}) async-start(), calls=%async_computation.10 | async-start | bytes 2359296 | tf_op jit(solution)/shard_map/all_gather | solution.py:427
  95.7 36.8 %all-to-all-start.4 = ((bf16[8,1424,128]{2,1,0:T(8,128)(2,1)}), bf16[8,1424,128]{2,1,0:T(8,128)(2,1)S(1)}, u32[]{:S(2)}, u32[]{:S(2)}) async-start(bf16[8,1424,128]{2,1,0:T(8,128)(2,1)} %attend.2), calls=%async_computation.4 | async-start | bytes 5832704 | tf_op jit(solution)/shard_map/all_to_all | solution.py:404
  135.4 12.7 %all-to-all-start.5 = ((bf16[8,80,128]{2,1,0:T(8,128)(2,1)}), bf16[8,80,128]{2,1,0:T(8,128)(2,1)S(1)}, u32[]{:S(2)}, u32[]{:S(2)}) async-start(bf16[8,80,128]{2,1,0:T(8,128)(2,1)} %merge_late.1), calls=%async_computation.5 | async-start | bytes 327680 | tf_op jit(solution)/shard_map/all_to_all | solution.py:404
  150.6 5.8 %copy-start.3 = (bf16[7168]{0:T(1024)(128)(2,1)S(1)}, bf16[7168]{0:T(1024)(128)(2,1)}, u32[]{:S(2)}) copy-start(bf16[7168]{0:T(1024)(128)(2,1)} %param.20) | copy-start | bytes 43012
  151.5 40.2 %copy-start = (bf16[1,7168,128]{2,1,0:T(8,128)(2,1)S(1)}, bf16[1,7168,128]{2,1,0:T(8,128)(2,1)}, u32[]{:S(2)}) copy-start(bf16[1,7168,128]{2,1,0:T(8,128)(2,1)} %param.23) | copy-start | bytes 5505028
  151.5 40.2 %copy-start.1 = (bf16[7168,8]{0,1:T(8,128)(2,1)S(1)}, bf16[7168,8]{0,1:T(8,128)(2,1)}, u32[]{:S(2)}) copy-start(bf16[7168,8]{0,1:T(8,128)(2,1)} %param.21) | copy-start | bytes 344068
  151.5 20.9 %all-to-all-start.6 = ((bf16[64,4,896]{2,1,0:T(4,128)(2,1)}), bf16[64,4,896]{2,1,0:T(4,128)(2,1)S(1)}, u32[]{:S(2)}, u32[]{:S(2)}) async-start(bf16[64,4,896]{2,1,0:T(4,128)(2,1)} %reshape.175), calls=%async_computation.6 | async-start | bytes 917504 | tf_op jit(solution)/shard_map/all_to_all | solution.py:404
  174.3 17.3 %all-to-all-start.7 = ((bf16[64,2,896]{2,1,0:T(2,128)(2,1)}), bf16[64,2,896]{2,1,0:T(2,128)(2,1)S(1)}, u32[]{:S(2)}, u32[]{:S(2)}) async-start(bf16[64,2,896]{2,1,0:T(2,128)(2,1)} %reshape.178), calls=%async_computation.7 | async-start | bytes 458752 | tf_op jit(solution)/shard_map/all_to_all | solution.py:404
Sparse Core Ops, SparseCore 0:
  24.6 50.7 all-gather.4
  81.2 38.1 all-gather.6

commit v3 on v2

--- a/solution.py
+++ b/solution.py
@@ -13,6 +13,7 @@
 bf16 = jnp.bfloat16
 VMEM_LIMIT = 16 * 1024 * 1024
 LANES = 128
+AHEAD = 4
 LOG2E = math.log2(math.e)
 TABLE = 16
 
@@ -29,17 +30,17 @@
     return pltpu.with_memory_space_constraint(x, pltpu.HBM)
 
 
-def attend_kernel(scale, n_ctx, n_exp, first, permuted, lengths, base, q_ref, k_ref, routes_ref, out_ref, *scratch):
-    stat_ref, buf_ref, table_ref, sems = scratch[:4]
+def attend_kernel(scale, n_ctx, n_exp, first, permuted, steps, lengths, base, q_far, k_far, routes_ref, out_ref, *scratch):
+    stat_ref, buf_ref, table_ref, sems, q_ref, k_ref, in_sems = scratch[:7]
     step = pl.program_id(0)
     slot = lax.rem(step, 2)
-    n_outer, unroll, per, depth = q_ref.shape
+    ahead, n_outer, unroll, per, depth = q_ref.shape
     rows = n_outer * per
     chunk = rows // n_exp
-    block = k_ref.shape[2]
+    block = k_ref.shape[3]
     tall = out_ref.shape[1] - TABLE
     lines = stat_ref.shape[2] // LANES
-    tiles = tall // (unroll * pl.num_programs(0) * chunk)
+    tiles = tall // (unroll * steps * chunk)
     width = tiles * LANES
 
     @pl.when(step == 0)
@@ -49,8 +50,30 @@
             per_pair = rows // (n_ctx * n_exp)
             to, frm = iota((rows, rows), 0), iota((rows, rows), 1)
             e, c, rest = to // chunk, (to % chunk) // per_pair, to % per_pair
-            scratch[4][...] = (frm == c * per + e * per_pair + rest).astype(bf16)
-
+            scratch[7][...] = (frm == c * per + e * per_pair + rest).astype(bf16)
+
+    def bring(where):
+        into = lax.rem(where, ahead)
+        mine, yours = pl.ds(where * unroll, unroll), pl.ds(first + where * unroll, unroll)
+        return (
+            pltpu.make_async_copy(q_far.at[:, mine], q_ref.at[into], in_sems.at[0, into]),
+            pltpu.make_async_copy(k_far.at[yours], k_ref.at[into], in_sems.at[1, into]),
+        )
+
+    @pl.when(step == 0)
+    def _():
+        for where in range(min(ahead - 1, steps)):
+            for copy in bring(where):
+                copy.start()
+
+    @pl.when(step + ahead - 1 < steps)
+    def _():
+        for copy in bring(step + ahead - 1):
+            copy.start()
+
+    for copy in bring(step):
+        copy.wait()
+    now = lax.rem(step, ahead)
     row = iota((rows, 1), 0)
     lane = iota((rows, block), 1)
     span = buf_ref.shape[2]
@@ -65,10 +88,10 @@
 
     for u in range(unroll):
         r = step * unroll + u
-        q = q_ref[:, u].reshape(rows, depth)
+        q = q_ref[now, :, u].reshape(rows, depth)
         if permuted:
-            q = dot(scratch[4][...], q).astype(bf16)
-        k = k_ref[u]
+            q = dot(scratch[7][...], q).astype(bf16)
+        k = k_ref[now, u]
         scores = dot(q, k) * (scale * LOG2E)
         visible = lane < lengths[first + r] + (row // 2) % 2 - base[0]
         masked = jnp.where(visible, scores, -1e30)
@@ -87,7 +110,7 @@
 
     leave(slot, step).start()
 
-    @pl.when(step == pl.num_programs(0) - 1)
+    @pl.when(step == steps - 1)
     def _():
         top, total = stat_ref[0], stat_ref[1]
         high = total.astype(bf16).astype(f32)
@@ -118,14 +141,14 @@
     tall = reqs * chunk * (lat // LANES) + TABLE
     wide = -(-reqs * chunk // LANES) * LANES
     return pl.pallas_call(
-        functools.partial(attend_kernel, scale, n_ctx, n_exp, first, permuted),
+        functools.partial(attend_kernel, scale, n_ctx, n_exp, first, permuted, reqs // unroll),
         out_shape=pltpu.HBM((n_exp, tall, LANES), bf16),
         grid_spec=pltpu.PrefetchScalarGridSpec(
             num_scalar_prefetch=2,
             grid=(reqs // unroll,),
             in_specs=[
-                pl.BlockSpec((n_outer, unroll, per, depth), lambda r, *_: (0, r, 0, 0)),
-                pl.BlockSpec((unroll, depth, block), lambda r, *_: (r + first // unroll, 0, 0)),
+                pl.BlockSpec(memory_space=pl.ANY),
+                pl.BlockSpec(memory_space=pl.ANY),
                 pl.BlockSpec((1, LANES), lambda r, *_: (0, 0)),
             ],
             out_specs=pl.BlockSpec(memory_space=pltpu.HBM),
@@ -134,6 +157,9 @@
                 pltpu.VMEM((2, n_exp, unroll * chunk * (lat // LANES), LANES), bf16),
                 pltpu.VMEM((n_exp, TABLE, LANES), bf16),
                 pltpu.SemaphoreType.DMA((3,)),
+                pltpu.VMEM((AHEAD, n_outer, unroll, per, depth), bf16),
+                pltpu.VMEM((AHEAD, unroll, depth, block), bf16),
+                pltpu.SemaphoreType.DMA((2, AHEAD)),
             ]
             + ([pltpu.VMEM((rows, rows), bf16)] if permuted else []),
         ),

time: 219 us -> 217 us (level)
  Pallas kernels: 29.7 us -> 26.8 us
    pallas_call x2, Pallas kernels: 21 us -> 18.1 us  [attend(): pl.pallas_call(functools.partial(attend_kernel, scale, n_ctx, n_exp, firs...]
  transfers between devices with their start and end apart: 9 -> 9, of which waited for: 7 -> 7; matrix products, arithmetic and copies ran while one was open for 2% -> 2% of each run, Pallas kernels for 10% -> 9%
where the time goes in v3:
time: 217 us; the launch traced here: 216 us
  waiting for transfers between devices  100 us (46%)
  blocking collectives  34.7 us (16%)
  starting transfers between devices  30 us (14%)
  Pallas kernels  26.8 us (12%)
  between operations  13.7 us (6%)
  local copies, waits for them, and re-layouts  7.01 us (3%)
  other arithmetic  2.67 us (1%)
    all_to_all x7, waiting for transfers between devices, swap(): return lax.all_to_all(x, axes, split_axis=0, concat_axis=0, tiled=True)  99.5 us
    all_to_all x2, blocking collectives, swap(): return lax.all_to_all(x, axes, split_axis=0, concat_axis=0, tiled=True)  34.7 us
    all_to_all x7, starting transfers between devices, swap(): return lax.all_to_all(x, axes, split_axis=0, concat_axis=0, tiled=True)  29.9 us
    pallas_call x2, Pallas kernels, attend(): pl.pallas_call(functools.partial(attend_kernel, scale, n_ctx, n_exp, firs...  18.1 us
  transfers between devices with their start and end apart: 9, of which 7 were waited for; matrix products, arithmetic and copies ran while one was open for 2% of the time, Pallas kernels for 9%

profile of v3, /device:TPU:4, one launch (start us, length us, event | category | flops | bytes accessed | tf_op | source)
XLA Modules:
  0.0 216.0 jit_solution(2171862209728004945)
XLA Ops:
  8.3 5.1 %all-to-all-start = ((bf16[8,44,576]{2,1,0:T(8,128)(2,1)}), bf16[8,44,576]{2,1,0:T(8,128)(2,1)S(1)}, u32[]{:S(2)}, u32[]{:S(2)}) async-start(bf16[8,44,576]{2,1,0:T(8,128)(2,1)} %broadcast_in_dim.20), calls=%async_computation | async-start | bytes 983040 | tf_op jit(solution)/shard_map/all_to_all | solution.py:430
  13.5 9.6 %all-to-all-done = bf16[8,44,576]{2,1,0:T(8,128)(2,1)S(1)} async-done(((bf16[8,44,576]{2,1,0:T(8,128)(2,1)}), bf16[8,44,576]{2,1,0:T(8,128)(2,1)S(1)}, u32[]{:S(2)}, u32[]{:S(2)}) %all-to-all-start) | async-done | bytes 405536 | tf_op jit(solution)/shard_map/all_to_all | solution.py:430
  23.4 1.0 reshape.171
  24.5 18.7 %all_to_all.45 = bf16[8,20,576]{2,1,0:T(8,128)(2,1)S(1)} all-to-all(bf16[8,20,576]{2,1,0:T(8,128)(2,1)S(1)} %broadcast_in_dim.21), channel_id=1, replica_groups=mesh['ctx'=8,'exp'=8,'req'=4] {'ctx'}, dimensions={0} | all-to-all | bytes 368640 | tf_op jit(solution)/shard_map/all_to_all | solution.py:430
  43.4 1.3 broadcast_in_dim.23
  44.7 3.7 %all-to-all-start.2 = ((bf16[8,160,576]{2,1,0:T(8,128)(2,1)}), bf16[8,160,576]{2,1,0:T(8,128)(2,1)S(1)}, u32[]{:S(2)}, u32[]{:S(2)}) async-start(bf16[8,160,576]{2,1,0:T(8,128)(2,1)} %broadcast_in_dim.23), calls=%async_computation.2 | async-start | bytes 3276800 | tf_op jit(solution)/shard_map/all_to_all | solution.py:430
  50.0 18.2 %all-to-all-done.2 = bf16[8,160,576]{2,1,0:T(8,128)(2,1)S(1)} async-done(((bf16[8,160,576]{2,1,0:T(8,128)(2,1)}), bf16[8,160,576]{2,1,0:T(8,128)(2,1)S(1)}, u32[]{:S(2)}, u32[]{:S(2)}) %all-to-all-start.2) | async-done | bytes 1474592 | tf_op jit(solution)/shard_map/all_to_all | solution.py:430
  68.1 6.1 %attend.3 = bf16[8,656,128]{2,1,0:T(8,128)(2,1)} custom-call(s32[16]{0:T(128)S(1)} %copy-done.2, s32[1]{0:T(128)} %bitcast.1.base, bf16[8,5,32,576]{3,2,1,0:T(8,128)(2,1)S(1)} %bitcast.28, bf16[16,576,512]{2,1,0:T(8,128)(2,1)} %bitcast.32, f32[1,128]{1,0:T(1,128)S(1)} %scatter.4.routes_ref), custom_call_target="tpu_custom_call" | custom-call | flops 1509949440 | bytes 5734400 | tf_op jit(solution)/shard_map/attend/pallas_call | solution.py:143
  74.2 3.6 %all-to-all-start.3 = ((bf16[8,656,128]{2,1,0:T(8,128)(2,1)}), bf16[8,656,128]{2,1,0:T(8,128)(2,1)S(1)}, u32[]{:S(2)}, u32[]{:S(2)}) async-start(bf16[8,656,128]{2,1,0:T(8,128)(2,1)} %attend.3), calls=%async_computation.3 | async-start | bytes 2686976 | tf_op jit(solution)/shard_map/all_to_all | solution.py:430
  78.5 12.0 %attend.2 = bf16[8,1424,128]{2,1,0:T(8,128)(2,1)} custom-call(s32[16]{0:T(128)S(1)} %copy-done.2, s32[1]{0:T(128)} %bitcast.1.base, bf16[8,11,32,576]{3,2,1,0:T(8,128)(2,1)} %bitcast.34, bf16[16,576,512]{2,1,0:T(8,128)(2,1)} %bitcast.33, f32[1,128]{1,0:T(1,128)S(1)} %scatter.4.routes_ref), custom_call_target="tpu_custom_call" | custom-call | flops 3321888768 | bytes 12615680 | tf_op jit(solution)/shard_map/attend/pallas_call | solution.py:143
  90.5 3.9 %all-to-all-done.3.in_ref = bf16[8,656,128]{2,1,0:T(8,128)(2,1)S(1)} async-done(((bf16[8,656,128]{2,1,0:T(8,128)(2,1)}), bf16[8,656,128]{2,1,0:T(8,128)(2,1)S(1)}, u32[]{:S(2)}, u32[]{:S(2)}) %all-to-all-start.3) | async-done | bytes 1343520 | tf_op jit(solution)/shard_map/all_to_all | solution.py:430
  94.9 3.7 %all-to-all-start.4 = ((bf16[8,1424,128]{2,1,0:T(8,128)(2,1)}), bf16[8,1424,128]{2,1,0:T(8,128)(2,1)S(1)}, u32[]{:S(2)}, u32[]{:S(2)}) async-start(bf16[8,1424,128]{2,1,0:T(8,128)(2,1)} %attend.2), calls=%async_computation.4 | async-start | bytes 5832704 | tf_op jit(solution)/shard_map/all_to_all | solution.py:430
  98.7 32.5 %all-to-all-done.4.in_ref = bf16[8,1424,128]{2,1,0:T(8,128)(2,1)S(1)} async-done(((bf16[8,1424,128]{2,1,0:T(8,128)(2,1)}), bf16[8,1424,128]{2,1,0:T(8,128)(2,1)S(1)}, u32[]{:S(2)}, u32[]{:S(2)}) %all-to-all-start.4) | async-done | bytes 2916384 | tf_op jit(solution)/shard_map/all_to_all | solution.py:430
  131.2 2.8 %merge_late.1 = bf16[8,80,128]{2,1,0:T(8,128)(2,1)} custom-call(bf16[160,512]{1,0:T(8,128)(2,1)S(1)} %get-tuple-element.34.early_ref, f32[8,160]{1,0:T(8,128)S(1)} %get-tuple-element.35.stat_ref, bf16[8,1424,128]{2,1,0:T(8,128)(2,1)S(1)} %all-to-all-done.4.in_ref, bf16[8,2,512,128]{3,2,1,0:T(8,128)(2,1)} %bitcast.35), custom_call_target="tpu_custom_call" | custom-call | tf_op jit(solution)/shard_map/merge_late/pallas_call | solution.py:266
  134.0 3.4 %all-to-all-start.5 = ((bf16[8,80,128]{2,1,0:T(8,128)(2,1)}), bf16[8,80,128]{2,1,0:T(8,128)(2,1)S(1)}, u32[]{:S(2)}, u32[]{:S(2)}) async-start(bf16[8,80,128]{2,1,0:T(8,128)(2,1)} %merge_late.1), calls=%async_computation.5 | async-start | bytes 327680 | tf_op jit(solution)/shard_map/all_to_all | solution.py:430
  137.5 9.3 %all-to-all-done.5.in_ref = bf16[8,80,128]{2,1,0:T(8,128)(2,1)S(1)} async-done(((bf16[8,80,128]{2,1,0:T(8,128)(2,1)}), bf16[8,80,128]{2,1,0:T(8,128)(2,1)S(1)}, u32[]{:S(2)}, u32[]{:S(2)}) %all-to-all-start.5) | async-done | bytes 163872 | tf_op jit(solution)/shard_map/all_to_all | solution.py:430
  146.8 2.5 %project.1 = bf16[8,32,896]{2,1,0:T(8,128)(2,1)S(1)} custom-call(s32[1]{0:T(128)} %bitcast.place, bf16[8,80,128]{2,1,0:T(8,128)(2,1)S(1)} %all-to-all-done.5.in_ref, bf16[256,7168]{1,0:T(8,128)(2,1)} %far_ref.1), custom_call_target="tpu_custom_call" | custom-call | tf_op jit(solution)/shard_map/project/pallas_call | solution.py:320
  149.3 0.9 reshape.175
  150.1 4.8 %all-to-all-start.6 = ((bf16[64,4,896]{2,1,0:T(4,128)(2,1)}), bf16[64,4,896]{2,1,0:T(4,128)(2,1)S(1)}, u32[]{:S(2)}, u32[]{:S(2)}) async-start(bf16[64,4,896]{2,1,0:T(4,128)(2,1)} %reshape.175), calls=%async_computation.6 | async-start | bytes 917504 | tf_op jit(solution)/shard_map/all_to_all | solution.py:430
  155.3 14.5 %all-to-all-done.6 = bf16[64,4,896]{2,1,0:T(4,128)(2,1)S(1)} async-done(((bf16[64,4,896]{2,1,0:T(4,128)(2,1)}), bf16[64,4,896]{2,1,0:T(4,128)(2,1)S(1)}, u32[]{:S(2)}, u32[]{:S(2)}) %all-to-all-start.6) | async-done | bytes 458784 | tf_op jit(solution)/shard_map/all_to_all | solution.py:430
  171.8 5.7 %all-to-all-start.7 = ((bf16[64,2,896]{2,1,0:T(2,128)(2,1)}), bf16[64,2,896]{2,1,0:T(2,128)(2,1)S(1)}, u32[]{:S(2)}, u32[]{:S(2)}) async-start(bf16[64,2,896]{2,1,0:T(2,128)(2,1)} %reshape.178), calls=%async_computation.7 | async-start | bytes 458752 | tf_op jit(solution)/shard_map/all_to_all | solution.py:430
  177.6 11.4 %all-to-all-done.7 = bf16[64,2,896]{2,1,0:T(2,128)(2,1)S(1)} async-done(((bf16[64,2,896]{2,1,0:T(2,128)(2,1)}), bf16[64,2,896]{2,1,0:T(2,128)(2,1)S(1)}, u32[]{:S(2)}, u32[]{:S(2)}) %all-to-all-start.7) | async-done | bytes 229408 | tf_op jit(solution)/shard_map/all_to_all | solution.py:430
  189.2 3.0 %experts.1 = bf16[8,16,896]{2,1,0:T(8,128)(2,1)S(1)} custom-call(s32[1]{0:T(128)} %bitcast.11.me, bf16[8,16,896]{2,1,0:T(8,128)(2,1)S(1)} %reshape.179.hid_ref, bf16[8,1,896]{2,1,0:T(2,128)(2,1)S(1)} %reshape.190.gain_ref, bf16[8,8,896]{2,1,0:T(8,128)(2,1)S(1)} %bitcast.30, s32[16,2]{1,0:T(8,128)S(1)} %bitcast.31, bf16[8,896,128]{2,1,0:T(8,128)(2,1)S(1)} %bitcast.29, ...), custom_call_target="tpu_custom_call" | custom-call | tf_op jit(solution)/shard_map/experts/pallas_call | solution.py:385
  192.3 16.0 %all_to_all.46 = bf16[64,2,896]{2,1,0:T(2,128)(2,1)S(1)} all-to-all(bf16[64,2,896]{2,1,0:T(2,128)(2,1)S(1)} %reshape.186), channel_id=1, replica_groups=mesh['ctx'=8,'exp'=8,'req'=4] {'ctx','exp'}, dimensions={0} | all-to-all | bytes 458752 | tf_op jit(solution)/shard_map/all_to_all | solution.py:430
  (61 shorter events, 8.7 us)
Async XLA Ops:
  6.5 6.9 %slice-start = ((bf16[16,2,2,576]{3,2,1,0:T(2,128)(2,1)}), bf16[5,2,2,576]{3,2,1,0:T(2,128)(2,1)S(1)}, s32[]{:S(2)}) async-start(bf16[16,2,2,576]{3,2,1,0:T(2,128)(2,1)} %param.14), calls=%async_computation.11 | async-start | bytes 51200 | tf_op jit(solution)/shard_map/slice | solution.py:441
  8.3 14.8 %all-to-all-start = ((bf16[8,44,576]{2,1,0:T(8,128)(2,1)}), bf16[8,44,576]{2,1,0:T(8,128)(2,1)S(1)}, u32[]{:S(2)}, u32[]{:S(2)}) async-start(bf16[8,44,576]{2,1,0:T(8,128)(2,1)} %broadcast_in_dim.20), calls=%async_computation | async-start | bytes 983040 | tf_op jit(solution)/shard_map/all_to_all | solution.py:430
  13.4 64.4 %all-gather.5.cloned.1.call-start = ((), (), s32[]{:S(2)}) async-start(), calls=%async_computation.9 | async-start | bytes 4055040 | tf_op jit(solution)/shard_map/all_gather | solution.py:442
  44.7 4.4 %copy-start.4 = (s32[4,2]{0,1:T(2,128)S(1)}, s32[4,2]{0,1:T(2,128)}, u32[]{:S(2)}) copy-start(s32[4,2]{0,1:T(2,128)} %param.22) | copy-start | bytes 100
  44.7 23.4 %copy-start.2 = (s32[16]{0:T(128)S(1)}, s32[16]{0:T(128)}, u32[]{:S(2)}) copy-start(s32[16]{0:T(128)} %lengths.3) | copy-start | bytes 196
  44.7 23.4 %all-to-all-start.2 = ((bf16[8,160,576]{2,1,0:T(8,128)(2,1)}), bf16[8,160,576]{2,1,0:T(8,128)(2,1)S(1)}, u32[]{:S(2)}, u32[]{:S(2)}) async-start(bf16[8,160,576]{2,1,0:T(8,128)(2,1)} %broadcast_in_dim.23), calls=%async_computation.2 | async-start | bytes 3276800 | tf_op jit(solution)/shard_map/all_to_all | solution.py:430
  74.2 20.3 %all-to-all-start.3 = ((bf16[8,656,128]{2,1,0:T(8,128)(2,1)}), bf16[8,656,128]{2,1,0:T(8,128)(2,1)S(1)}, u32[]{:S(2)}, u32[]{:S(2)}) async-start(bf16[8,656,128]{2,1,0:T(8,128)(2,1)} %attend.3), calls=%async_computation.3 | async-start | bytes 2686976 | tf_op jit(solution)/shard_map/all_to_all | solution.py:430
  77.8 53.4 %all-gather.7.cloned.1.call-start = ((), (), s32[]{:S(2)}) async-start(), calls=%async_computation.10 | async-start | bytes 2359296 | tf_op jit(solution)/shard_map/all_gather | solution.py:453
  94.9 36.3 %all-to-all-start.4 = ((bf16[8,1424,128]{2,1,0:T(8,128)(2,1)}), bf16[8,1424,128]{2,1,0:T(8,128)(2,1)S(1)}, u32[]{:S(2)}, u32[]{:S(2)}) async-start(bf16[8,1424,128]{2,1,0:T(8,128)(2,1)} %attend.2), calls=%async_computation.4 | async-start | bytes 5832704 | tf_op jit(solution)/shard_map/all_to_all | solution.py:430
  134.0 12.7 %all-to-all-start.5 = ((bf16[8,80,128]{2,1,0:T(8,128)(2,1)}), bf16[8,80,128]{2,1,0:T(8,128)(2,1)S(1)}, u32[]{:S(2)}, u32[]{:S(2)}) async-start(bf16[8,80,128]{2,1,0:T(8,128)(2,1)} %merge_late.1), calls=%async_computation.5 | async-start | bytes 327680 | tf_op jit(solution)/shard_map/all_to_all | solution.py:430
  149.3 5.8 %copy-start.3 = (bf16[7168]{0:T(1024)(128)(2,1)S(1)}, bf16[7168]{0:T(1024)(128)(2,1)}, u32[]{:S(2)}) copy-start(bf16[7168]{0:T(1024)(128)(2,1)} %param.20) | copy-start | bytes 43012
  150.1 39.0 %copy-start = (bf16[1,7168,128]{2,1,0:T(8,128)(2,1)S(1)}, bf16[1,7168,128]{2,1,0:T(8,128)(2,1)}, u32[]{:S(2)}) copy-start(bf16[1,7168,128]{2,1,0:T(8,128)(2,1)} %param.23) | copy-start | bytes 5505028
  150.1 39.0 %copy-start.1 = (bf16[7168,8]{0,1:T(8,128)(2,1)S(1)}, bf16[7168,8]{0,1:T(8,128)(2,1)}, u32[]{:S(2)}) copy-start(bf16[7168,8]{0,1:T(8,128)(2,1)} %param.21) | copy-start | bytes 344068
  150.1 19.7 %all-to-all-start.6 = ((bf16[64,4,896]{2,1,0:T(4,128)(2,1)}), bf16[64,4,896]{2,1,0:T(4,128)(2,1)S(1)}, u32[]{:S(2)}, u32[]{:S(2)}) async-start(bf16[64,4,896]{2,1,0:T(4,128)(2,1)} %reshape.175), calls=%async_computation.6 | async-start | bytes 917504 | tf_op jit(solution)/shard_map/all_to_all | solution.py:430
  171.8 17.3 %all-to-all-start.7 = ((bf16[64,2,896]{2,1,0:T(2,128)(2,1)}), bf16[64,2,896]{2,1,0:T(2,128)(2,1)S(1)}, u32[]{:S(2)}, u32[]{:S(2)}) async-start(bf16[64,2,896]{2,1,0:T(2,128)(2,1)} %reshape.178), calls=%async_computation.7 | async-start | bytes 458752 | tf_op jit(solution)/shard_map/all_to_all | solution.py:430
Sparse Core Ops, SparseCore 0:
  24.6 50.7 all-gather.4
  80.4 38.0 all-gather.6

commit v4 on v3

--- a/solution.py
+++ b/solution.py
@@ -280,7 +280,8 @@
 def project_kernel(place, in_ref, far_ref, out_ref, proj_ref, sum_ref, sems):
     sources, tall, vdim = in_ref.shape
     own = tall - TABLE
-    blocks, rows, cols = out_ref.shape
+    blocks, rows, cols = sum_ref.shape
+    each = out_ref.shape[0] // blocks
     heads = own // rows
     copies = []
     for h in range(heads):
@@ -308,20 +309,21 @@
             if h < heads - 1:
                 sum_ref[c] = term
             else:
-                out_ref[c] = term.astype(bf16)
-
-
-def project(arrived, place, out_proj, n_ctx):
+                out_ref[c * each : (c + 1) * each] = term.reshape(each, rows // each, cols).astype(bf16)
+
+
+def project(arrived, place, out_proj, n_ctx, n_exp):
     sources, tall, vdim = arrived.shape
     depth, model = out_proj.shape
     cols = model // n_ctx
     rows = (tall - TABLE) * vdim // depth
+    shape = (n_ctx * n_exp, rows // n_exp, cols)
     vmem = pl.BlockSpec(memory_space=pltpu.VMEM)
     return pl.pallas_call(
         project_kernel,
-        out_shape=jax.ShapeDtypeStruct((n_ctx, rows, cols), bf16),
+        out_shape=pltpu.HBM(shape, bf16),
         in_specs=[pl.BlockSpec(memory_space=pltpu.SMEM), vmem, pl.BlockSpec(memory_space=pltpu.HBM)],
-        out_specs=vmem,
+        out_specs=pl.BlockSpec(shape, lambda: (0, 0, 0)),
         scratch_shapes=[
             pltpu.VMEM(out_proj.shape, bf16),
             pltpu.VMEM((n_ctx, rows, cols), f32),
@@ -459,12 +461,13 @@
     sent, sums = lax.optimization_barrier((sent, sums))
     arrived = swap(sent, "exp")
     arrived = swap(merge_late(sums, stats, arrived, all_up, reqs - early), "ctx")
-    terms = project(arrived, ctx.reshape(1), out_proj, n_ctx)
-
-    terms = swap(terms.reshape(n_all, own_rows, cols), everyone)
+    own = lax.dynamic_slice_in_dim(residual, ctx * cols, cols, 1).astype(f32)
+    arrived, own = lax.optimization_barrier((arrived, own))
+    terms = project(arrived, ctx.reshape(1), out_proj, n_ctx, n_exp)
+
+    terms = swap(terms, everyone)
     attention = jnp.sum(terms.astype(f32), axis=0)
-    own = lax.dynamic_slice_in_dim(residual, ctx * cols, cols, 1)
-    hidden = (own.astype(f32) + attention).astype(bf16)
+    hidden = (own + attention).astype(bf16)
 
     slots = max(2, own_rows * top // experts)
     before = jnp.tril(jnp.ones((own_rows, own_rows), jnp.int32), -1)

time: 217 us -> 216 us (level)
  no operation moved by 1% of the time
where the time goes in v4:
time: 216 us; the launch traced here: 215 us
  waiting for transfers between devices  99.5 us (46%)
  blocking collectives  34.7 us (16%)
  starting transfers between devices  30 us (14%)
  Pallas kernels  27.6 us (13%)
  between operations  13.7 us (6%)
  local copies, waits for them, and re-layouts  6.14 us (3%)
  other arithmetic  2.68 us (1%)
    all_to_all x7, waiting for transfers between devices, swap(): return lax.all_to_all(x, axes, split_axis=0, concat_axis=0, tiled=True)  98.8 us
    all_to_all x2, blocking collectives, swap(): return lax.all_to_all(x, axes, split_axis=0, concat_axis=0, tiled=True)  34.7 us
    all_to_all x7, starting transfers between devices, swap(): return lax.all_to_all(x, axes, split_axis=0, concat_axis=0, tiled=True)  29.9 us
    pallas_call x2, Pallas kernels, attend(): pl.pallas_call(functools.partial(attend_kernel, scale, n_ctx, n_exp, firs...  18.1 us
  transfers between devices with their start and end apart: 9, of which 7 were waited for; matrix products, arithmetic and copies ran while one was open for 2% of the time, Pallas kernels for 9%

profile of v4, /device:TPU:4, one launch (start us, length us, event | category | flops | bytes accessed | tf_op | source)
XLA Modules:
  0.0 215.2 jit_solution(8092786065359455945)
XLA Ops:
  6.5 0.9 slice.31
  8.3 5.1 %all-to-all-start = ((bf16[8,44,576]{2,1,0:T(8,128)(2,1)}), bf16[8,44,576]{2,1,0:T(8,128)(2,1)S(1)}, u32[]{:S(2)}, u32[]{:S(2)}) async-start(bf16[8,44,576]{2,1,0:T(8,128)(2,1)} %broadcast_in_dim.20), calls=%async_computation | async-start | bytes 983040 | tf_op jit(solution)/shard_map/all_to_all | solution.py:432
  13.5 9.6 %all-to-all-done = bf16[8,44,576]{2,1,0:T(8,128)(2,1)S(1)} async-done(((bf16[8,44,576]{2,1,0:T(8,128)(2,1)}), bf16[8,44,576]{2,1,0:T(8,128)(2,1)S(1)}, u32[]{:S(2)}, u32[]{:S(2)}) %all-to-all-start) | async-done | bytes 405536 | tf_op jit(solution)/shard_map/all_to_all | solution.py:432
  23.4 1.0 reshape.167
  24.5 18.7 %all_to_all.45 = bf16[8,20,576]{2,1,0:T(8,128)(2,1)S(1)} all-to-all(bf16[8,20,576]{2,1,0:T(8,128)(2,1)S(1)} %broadcast_in_dim.21), channel_id=1, replica_groups=mesh['ctx'=8,'exp'=8,'req'=4] {'ctx'}, dimensions={0} | all-to-all | bytes 368640 | tf_op jit(solution)/shard_map/all_to_all | solution.py:432
  43.4 1.3 broadcast_in_dim.23
  44.7 3.7 %all-to-all-start.2 = ((bf16[8,160,576]{2,1,0:T(8,128)(2,1)}), bf16[8,160,576]{2,1,0:T(8,128)(2,1)S(1)}, u32[]{:S(2)}, u32[]{:S(2)}) async-start(bf16[8,160,576]{2,1,0:T(8,128)(2,1)} %broadcast_in_dim.23), calls=%async_computation.2 | async-start | bytes 3276800 | tf_op jit(solution)/shard_map/all_to_all | solution.py:432
  50.0 18.2 %all-to-all-done.2 = bf16[8,160,576]{2,1,0:T(8,128)(2,1)S(1)} async-done(((bf16[8,160,576]{2,1,0:T(8,128)(2,1)}), bf16[8,160,576]{2,1,0:T(8,128)(2,1)S(1)}, u32[]{:S(2)}, u32[]{:S(2)}) %all-to-all-start.2) | async-done | bytes 1474592 | tf_op jit(solution)/shard_map/all_to_all | solution.py:432
  68.1 6.1 %attend.3 = bf16[8,656,128]{2,1,0:T(8,128)(2,1)} custom-call(s32[16]{0:T(128)S(1)} %copy-done.2, s32[1]{0:T(128)} %bitcast.base, bf16[8,5,32,576]{3,2,1,0:T(8,128)(2,1)S(1)} %bitcast.28, bf16[16,576,512]{2,1,0:T(8,128)(2,1)} %bitcast.32, f32[1,128]{1,0:T(1,128)S(1)} %scatter.4.routes_ref), custom_call_target="tpu_custom_call" | custom-call | flops 1509949440 | bytes 5734400 | tf_op jit(solution)/shard_map/attend/pallas_call | solution.py:143
  74.2 3.6 %all-to-all-start.3 = ((bf16[8,656,128]{2,1,0:T(8,128)(2,1)}), bf16[8,656,128]{2,1,0:T(8,128)(2,1)S(1)}, u32[]{:S(2)}, u32[]{:S(2)}) async-start(bf16[8,656,128]{2,1,0:T(8,128)(2,1)} %attend.3), calls=%async_computation.3 | async-start | bytes 2686976 | tf_op jit(solution)/shard_map/all_to_all | solution.py:432
  78.5 12.0 %attend.2 = bf16[8,1424,128]{2,1,0:T(8,128)(2,1)} custom-call(s32[16]{0:T(128)S(1)} %copy-done.2, s32[1]{0:T(128)} %bitcast.base, bf16[8,11,32,576]{3,2,1,0:T(8,128)(2,1)} %bitcast.34, bf16[16,576,512]{2,1,0:T(8,128)(2,1)} %bitcast.33, f32[1,128]{1,0:T(1,128)S(1)} %scatter.4.routes_ref), custom_call_target="tpu_custom_call" | custom-call | flops 3321888768 | bytes 12615680 | tf_op jit(solution)/shard_map/attend/pallas_call | solution.py:143
  90.5 3.9 %all-to-all-done.3.in_ref = bf16[8,656,128]{2,1,0:T(8,128)(2,1)S(1)} async-done(((bf16[8,656,128]{2,1,0:T(8,128)(2,1)}), bf16[8,656,128]{2,1,0:T(8,128)(2,1)S(1)}, u32[]{:S(2)}, u32[]{:S(2)}) %all-to-all-start.3) | async-done | bytes 1343520 | tf_op jit(solution)/shard_map/all_to_all | solution.py:432
  94.9 3.7 %all-to-all-start.4 = ((bf16[8,1424,128]{2,1,0:T(8,128)(2,1)}), bf16[8,1424,128]{2,1,0:T(8,128)(2,1)S(1)}, u32[]{:S(2)}, u32[]{:S(2)}) async-start(bf16[8,1424,128]{2,1,0:T(8,128)(2,1)} %attend.2), calls=%async_computation.4 | async-start | bytes 5832704 | tf_op jit(solution)/shard_map/all_to_all | solution.py:432
  99.4 31.8 %all-to-all-done.4.in_ref = bf16[8,1424,128]{2,1,0:T(8,128)(2,1)S(1)} async-done(((bf16[8,1424,128]{2,1,0:T(8,128)(2,1)}), bf16[8,1424,128]{2,1,0:T(8,128)(2,1)S(1)}, u32[]{:S(2)}, u32[]{:S(2)}) %all-to-all-start.4) | async-done | bytes 2916384 | tf_op jit(solution)/shard_map/all_to_all | solution.py:432
  131.2 2.8 %merge_late.1 = bf16[8,80,128]{2,1,0:T(8,128)(2,1)} custom-call(bf16[160,512]{1,0:T(8,128)(2,1)S(1)} %get-tuple-element.36.early_ref, f32[8,160]{1,0:T(8,128)S(1)} %get-tuple-element.37.stat_ref, bf16[8,1424,128]{2,1,0:T(8,128)(2,1)S(1)} %all-to-all-done.4.in_ref, bf16[8,2,512,128]{3,2,1,0:T(8,128)(2,1)} %bitcast.35), custom_call_target="tpu_custom_call" | custom-call | tf_op jit(solution)/shard_map/merge_late/pallas_call | solution.py:266
  134.0 3.4 %all-to-all-start.5 = ((bf16[8,80,128]{2,1,0:T(8,128)(2,1)}), bf16[8,80,128]{2,1,0:T(8,128)(2,1)S(1)}, u32[]{:S(2)}, u32[]{:S(2)}) async-start(bf16[8,80,128]{2,1,0:T(8,128)(2,1)} %merge_late.1), calls=%async_computation.5 | async-start | bytes 327680 | tf_op jit(solution)/shard_map/all_to_all | solution.py:432
  137.5 9.3 %all-to-all-done.5.in_ref = bf16[8,80,128]{2,1,0:T(8,128)(2,1)S(1)} async-done(((bf16[8,80,128]{2,1,0:T(8,128)(2,1)}), bf16[8,80,128]{2,1,0:T(8,128)(2,1)S(1)}, u32[]{:S(2)}, u32[]{:S(2)}) %all-to-all-start.5) | async-done | bytes 163872 | tf_op jit(solution)/shard_map/all_to_all | solution.py:432
  146.8 3.3 %project.1 = bf16[64,4,896]{2,1,0:T(4,128)(2,1)} custom-call(s32[1]{0:T(128)} %bitcast.9.place, bf16[8,80,128]{2,1,0:T(8,128)(2,1)S(1)} %all-to-all-done.5.in_ref, bf16[256,7168]{1,0:T(8,128)(2,1)} %far_ref.1), custom_call_target="tpu_custom_call" | custom-call | tf_op jit(solution)/shard_map/project/pallas_call | solution.py:322
  150.1 4.8 %all-to-all-start.6 = ((bf16[64,4,896]{2,1,0:T(4,128)(2,1)}), bf16[64,4,896]{2,1,0:T(4,128)(2,1)S(1)}, u32[]{:S(2)}, u32[]{:S(2)}) async-start(bf16[64,4,896]{2,1,0:T(4,128)(2,1)} %project.1), calls=%async_computation.6 | async-start | bytes 917504 | tf_op jit(solution)/shard_map/all_to_all | solution.py:432
  155.3 14.5 %all-to-all-done.6 = bf16[64,4,896]{2,1,0:T(4,128)(2,1)S(1)} async-done(((bf16[64,4,896]{2,1,0:T(4,128)(2,1)}), bf16[64,4,896]{2,1,0:T(4,128)(2,1)S(1)}, u32[]{:S(2)}, u32[]{:S(2)}) %all-to-all-start.6) | async-done | bytes 458784 | tf_op jit(solution)/shard_map/all_to_all | solution.py:432
  171.0 5.7 %all-to-all-start.7 = ((bf16[64,2,896]{2,1,0:T(2,128)(2,1)}), bf16[64,2,896]{2,1,0:T(2,128)(2,1)S(1)}, u32[]{:S(2)}, u32[]{:S(2)}) async-start(bf16[64,2,896]{2,1,0:T(2,128)(2,1)} %reshape.174), calls=%async_computation.7 | async-start | bytes 458752 | tf_op jit(solution)/shard_map/all_to_all | solution.py:432
  176.9 11.4 %all-to-all-done.7 = bf16[64,2,896]{2,1,0:T(2,128)(2,1)S(1)} async-done(((bf16[64,2,896]{2,1,0:T(2,128)(2,1)}), bf16[64,2,896]{2,1,0:T(2,128)(2,1)S(1)}, u32[]{:S(2)}, u32[]{:S(2)}) %all-to-all-start.7) | async-done | bytes 229408 | tf_op jit(solution)/shard_map/all_to_all | solution.py:432
  188.4 3.0 %experts.1 = bf16[8,16,896]{2,1,0:T(8,128)(2,1)S(1)} custom-call(s32[1]{0:T(128)} %bitcast.11.me, bf16[8,16,896]{2,1,0:T(8,128)(2,1)S(1)} %reshape.175.hid_ref, bf16[8,1,896]{2,1,0:T(2,128)(2,1)S(1)} %reshape.186.gain_ref, bf16[8,8,896]{2,1,0:T(8,128)(2,1)S(1)} %bitcast.30, s32[16,2]{1,0:T(8,128)S(1)} %bitcast.31, bf16[8,896,128]{2,1,0:T(8,128)(2,1)S(1)} %bitcast.29, ...), custom_call_target="tpu_custom_call" | custom-call | tf_op jit(solution)/shard_map/experts/pallas_call | solution.py:387
  191.5 16.0 %all_to_all.46 = bf16[64,2,896]{2,1,0:T(2,128)(2,1)S(1)} all-to-all(bf16[64,2,896]{2,1,0:T(2,128)(2,1)S(1)} %reshape.182), channel_id=1, replica_groups=mesh['ctx'=8,'exp'=8,'req'=4] {'ctx','exp'}, dimensions={0} | all-to-all | bytes 458752 | tf_op jit(solution)/shard_map/all_to_all | solution.py:432
  (61 shorter events, 7.9 us)
Async XLA Ops:
  6.5 6.9 %slice-start = ((bf16[16,2,2,576]{3,2,1,0:T(2,128)(2,1)}), bf16[5,2,2,576]{3,2,1,0:T(2,128)(2,1)S(1)}, s32[]{:S(2)}) async-start(bf16[16,2,2,576]{3,2,1,0:T(2,128)(2,1)} %param.14), calls=%async_computation.11 | async-start | bytes 51200 | tf_op jit(solution)/shard_map/slice | solution.py:443
  8.3 14.8 %all-to-all-start = ((bf16[8,44,576]{2,1,0:T(8,128)(2,1)}), bf16[8,44,576]{2,1,0:T(8,128)(2,1)S(1)}, u32[]{:S(2)}, u32[]{:S(2)}) async-start(bf16[8,44,576]{2,1,0:T(8,128)(2,1)} %broadcast_in_dim.20), calls=%async_computation | async-start | bytes 983040 | tf_op jit(solution)/shard_map/all_to_all | solution.py:432
  13.4 64.4 %all-gather.5.cloned.1.call-start = ((), (), s32[]{:S(2)}) async-start(), calls=%async_computation.9 | async-start | bytes 4055040 | tf_op jit(solution)/shard_map/all_gather | solution.py:444
  44.7 4.4 %copy-start.4 = (s32[4,2]{0,1:T(2,128)S(1)}, s32[4,2]{0,1:T(2,128)}, u32[]{:S(2)}) copy-start(s32[4,2]{0,1:T(2,128)} %param.22) | copy-start | bytes 100
  44.7 23.4 %copy-start.2 = (s32[16]{0:T(128)S(1)}, s32[16]{0:T(128)}, u32[]{:S(2)}) copy-start(s32[16]{0:T(128)} %lengths.3) | copy-start | bytes 196
  44.7 23.4 %all-to-all-start.2 = ((bf16[8,160,576]{2,1,0:T(8,128)(2,1)}), bf16[8,160,576]{2,1,0:T(8,128)(2,1)S(1)}, u32[]{:S(2)}, u32[]{:S(2)}) async-start(bf16[8,160,576]{2,1,0:T(8,128)(2,1)} %broadcast_in_dim.23), calls=%async_computation.2 | async-start | bytes 3276800 | tf_op jit(solution)/shard_map/all_to_all | solution.py:432
  74.2 20.3 %all-to-all-start.3 = ((bf16[8,656,128]{2,1,0:T(8,128)(2,1)}), bf16[8,656,128]{2,1,0:T(8,128)(2,1)S(1)}, u32[]{:S(2)}, u32[]{:S(2)}) async-start(bf16[8,656,128]{2,1,0:T(8,128)(2,1)} %attend.3), calls=%async_computation.3 | async-start | bytes 2686976 | tf_op jit(solution)/shard_map/all_to_all | solution.py:432
  77.8 53.4 %all-gather.7.cloned.1.call-start = ((), (), s32[]{:S(2)}) async-start(), calls=%async_computation.10 | async-start | bytes 2359296 | tf_op jit(solution)/shard_map/all_gather | solution.py:455
  94.9 36.3 %all-to-all-start.4 = ((bf16[8,1424,128]{2,1,0:T(8,128)(2,1)}), bf16[8,1424,128]{2,1,0:T(8,128)(2,1)S(1)}, u32[]{:S(2)}, u32[]{:S(2)}) async-start(bf16[8,1424,128]{2,1,0:T(8,128)(2,1)} %attend.2), calls=%async_computation.4 | async-start | bytes 5832704 | tf_op jit(solution)/shard_map/all_to_all | solution.py:432
  134.0 12.7 %all-to-all-start.5 = ((bf16[8,80,128]{2,1,0:T(8,128)(2,1)}), bf16[8,80,128]{2,1,0:T(8,128)(2,1)S(1)}, u32[]{:S(2)}, u32[]{:S(2)}) async-start(bf16[8,80,128]{2,1,0:T(8,128)(2,1)} %merge_late.1), calls=%async_computation.5 | async-start | bytes 327680 | tf_op jit(solution)/shard_map/all_to_all | solution.py:432
  146.8 8.3 %copy-start.3 = (bf16[7168]{0:T(1024)(128)(2,1)S(1)}, bf16[7168]{0:T(1024)(128)(2,1)}, u32[]{:S(2)}) copy-start(bf16[7168]{0:T(1024)(128)(2,1)} %param.20) | copy-start | bytes 43012
  150.0 38.4 %copy-start = (bf16[1,7168,128]{2,1,0:T(8,128)(2,1)S(1)}, bf16[1,7168,128]{2,1,0:T(8,128)(2,1)}, u32[]{:S(2)}) copy-start(bf16[1,7168,128]{2,1,0:T(8,128)(2,1)} %param.23) | copy-start | bytes 5505028
  150.0 38.4 %copy-start.1 = (bf16[7168,8]{0,1:T(8,128)(2,1)S(1)}, bf16[7168,8]{0,1:T(8,128)(2,1)}, u32[]{:S(2)}) copy-start(bf16[7168,8]{0,1:T(8,128)(2,1)} %param.21) | copy-start | bytes 344068
  150.1 19.7 %all-to-all-start.6 = ((bf16[64,4,896]{2,1,0:T(4,128)(2,1)}), bf16[64,4,896]{2,1,0:T(4,128)(2,1)S(1)}, u32[]{:S(2)}, u32[]{:S(2)}) async-start(bf16[64,4,896]{2,1,0:T(4,128)(2,1)} %project.1), calls=%async_computation.6 | async-start | bytes 917504 | tf_op jit(solution)/shard_map/all_to_all | solution.py:432
  171.0 17.3 %all-to-all-start.7 = ((bf16[64,2,896]{2,1,0:T(2,128)(2,1)}), bf16[64,2,896]{2,1,0:T(2,128)(2,1)S(1)}, u32[]{:S(2)}, u32[]{:S(2)}) async-start(bf16[64,2,896]{2,1,0:T(2,128)(2,1)} %reshape.174), calls=%async_computation.7 | async-start | bytes 458752 | tf_op jit(solution)/shard_map/all_to_all | solution.py:432
Sparse Core Ops, SparseCore 0:
  24.6 50.7 all-gather.4
  80.4 38.0 all-gather.6

commit v5 on v4

--- a/solution.py
+++ b/solution.py
@@ -379,14 +379,16 @@
     active = (gate / (1.0 + jnp.exp(-gate)) * up).astype(bf16)
     for c in range(blocks):
         got = dot(active, down_ref[:, c * cols : (c + 1) * cols])
-        out_ref[c] = (got * weight).astype(bf16)
-
-
-def experts_here(hidden, gain, router, routes, me, gate, up, down):
+        each = out_ref.shape[0] // blocks
+        got = (got * weight).reshape(each, rows // each, cols)
+        out_ref[c * each : (c + 1) * each] = got.astype(bf16)
+
+
+def experts_here(shape, hidden, gain, router, routes, me, gate, up, down):
     vmem = pl.BlockSpec(memory_space=pltpu.VMEM)
     return pl.pallas_call(
         expert_kernel,
-        out_shape=jax.ShapeDtypeStruct(hidden.shape, bf16),
+        out_shape=jax.ShapeDtypeStruct(shape, bf16),
         in_specs=[pl.BlockSpec(memory_space=pltpu.SMEM)]
         + [vmem] * 5
         + [pl.BlockSpec(memory_space=pltpu.HBM)] * 2,
@@ -487,6 +489,7 @@
     taken = (slot_of(named, 1)[:, None, :] == jnp.arange(slots)[None, :, None]).astype(jnp.int32)
     slot_routes = jnp.sum(taken[..., None] * all_routes[:, None], axis=2).reshape(n_exp * slots, top)
     mixed = experts_here(
+        (n_all, slots, cols),
         rows.reshape(n_ctx, n_exp * slots, cols),
         norm_gain.reshape(n_ctx, 1, cols),
         router.T.reshape(experts, n_ctx, cols).transpose(1, 0, 2),
@@ -496,7 +499,7 @@
         expert_up.reshape(n_ctx, cols, -1),
         expert_down[0],
     )
-    mixed = swap(mixed.reshape(n_all, slots, cols), everyone)
+    mixed = swap(mixed, everyone)
     mixture = dot(place, mixed.reshape(n_all * slots, cols))
     return (hidden.astype(f32) + mixture).astype(bf16)
 

time: 216 us -> 216 us (level)
  no operation moved by 1% of the time
where the time goes in v5:
time: 216 us; the launch traced here: 215 us
  waiting for transfers between devices  99.5 us (46%)
  blocking collectives  34.7 us (16%)
  starting transfers between devices  30 us (14%)
  Pallas kernels  27.6 us (13%)
  between operations  13.7 us (6%)
  local copies, waits for them, and re-layouts  6.05 us (3%)
  other arithmetic  2.68 us (1%)
    all_to_all x7, waiting for transfers between devices, swap(): return lax.all_to_all(x, axes, split_axis=0, concat_axis=0, tiled=True)  98.8 us
    all_to_all x2, blocking collectives, swap(): return lax.all_to_all(x, axes, split_axis=0, concat_axis=0, tiled=True)  34.7 us
    all_to_all x7, starting transfers between devices, swap(): return lax.all_to_all(x, axes, split_axis=0, concat_axis=0, tiled=True)  29.9 us
    pallas_call x2, Pallas kernels, attend(): pl.pallas_call(functools.partial(attend_kernel, scale, n_ctx, n_exp, firs...  18.1 us
  transfers between devices with their start and end apart: 9, of which 7 were waited for; matrix products, arithmetic and copies ran while one was open for 2% of the time, Pallas kernels for 9%

profile of v5, /device:TPU:4, one launch (start us, length us, event | category | flops | bytes accessed | tf_op | source)
XLA Modules:
  0.0 215.2 jit_solution(13065324758148153179)
XLA Ops:
  6.5 0.9 slice.31
  8.3 5.1 %all-to-all-start = ((bf16[8,44,576]{2,1,0:T(8,128)(2,1)}), bf16[8,44,576]{2,1,0:T(8,128)(2,1)S(1)}, u32[]{:S(2)}, u32[]{:S(2)}) async-start(bf16[8,44,576]{2,1,0:T(8,128)(2,1)} %broadcast_in_dim.20), calls=%async_computation | async-start | bytes 983040 | tf_op jit(solution)/shard_map/all_to_all | solution.py:434
  13.5 9.6 %all-to-all-done = bf16[8,44,576]{2,1,0:T(8,128)(2,1)S(1)} async-done(((bf16[8,44,576]{2,1,0:T(8,128)(2,1)}), bf16[8,44,576]{2,1,0:T(8,128)(2,1)S(1)}, u32[]{:S(2)}, u32[]{:S(2)}) %all-to-all-start) | async-done | bytes 405536 | tf_op jit(solution)/shard_map/all_to_all | solution.py:434
  23.4 1.0 reshape.164
  24.5 18.7 %all_to_all.45 = bf16[8,20,576]{2,1,0:T(8,128)(2,1)S(1)} all-to-all(bf16[8,20,576]{2,1,0:T(8,128)(2,1)S(1)} %broadcast_in_dim.21), channel_id=1, replica_groups=mesh['ctx'=8,'exp'=8,'req'=4] {'ctx'}, dimensions={0} | all-to-all | bytes 368640 | tf_op jit(solution)/shard_map/all_to_all | solution.py:434
  43.4 1.3 broadcast_in_dim.23
  44.7 3.7 %all-to-all-start.2 = ((bf16[8,160,576]{2,1,0:T(8,128)(2,1)}), bf16[8,160,576]{2,1,0:T(8,128)(2,1)S(1)}, u32[]{:S(2)}, u32[]{:S(2)}) async-start(bf16[8,160,576]{2,1,0:T(8,128)(2,1)} %broadcast_in_dim.23), calls=%async_computation.2 | async-start | bytes 3276800 | tf_op jit(solution)/shard_map/all_to_all | solution.py:434
  50.0 18.2 %all-to-all-done.2 = bf16[8,160,576]{2,1,0:T(8,128)(2,1)S(1)} async-done(((bf16[8,160,576]{2,1,0:T(8,128)(2,1)}), bf16[8,160,576]{2,1,0:T(8,128)(2,1)S(1)}, u32[]{:S(2)}, u32[]{:S(2)}) %all-to-all-start.2) | async-done | bytes 1474592 | tf_op jit(solution)/shard_map/all_to_all | solution.py:434
  68.1 6.1 %attend.3 = bf16[8,656,128]{2,1,0:T(8,128)(2,1)} custom-call(s32[16]{0:T(128)S(1)} %copy-done.2, s32[1]{0:T(128)} %bitcast.base, bf16[8,5,32,576]{3,2,1,0:T(8,128)(2,1)S(1)} %bitcast.28, bf16[16,576,512]{2,1,0:T(8,128)(2,1)} %bitcast.32, f32[1,128]{1,0:T(1,128)S(1)} %scatter.4.routes_ref), custom_call_target="tpu_custom_call" | custom-call | flops 1509949440 | bytes 5734400 | tf_op jit(solution)/shard_map/attend/pallas_call | solution.py:143
  74.2 3.6 %all-to-all-start.3 = ((bf16[8,656,128]{2,1,0:T(8,128)(2,1)}), bf16[8,656,128]{2,1,0:T(8,128)(2,1)S(1)}, u32[]{:S(2)}, u32[]{:S(2)}) async-start(bf16[8,656,128]{2,1,0:T(8,128)(2,1)} %attend.3), calls=%async_computation.3 | async-start | bytes 2686976 | tf_op jit(solution)/shard_map/all_to_all | solution.py:434
  78.5 12.0 %attend.2 = bf16[8,1424,128]{2,1,0:T(8,128)(2,1)} custom-call(s32[16]{0:T(128)S(1)} %copy-done.2, s32[1]{0:T(128)} %bitcast.base, bf16[8,11,32,576]{3,2,1,0:T(8,128)(2,1)} %bitcast.34, bf16[16,576,512]{2,1,0:T(8,128)(2,1)} %bitcast.33, f32[1,128]{1,0:T(1,128)S(1)} %scatter.4.routes_ref), custom_call_target="tpu_custom_call" | custom-call | flops 3321888768 | bytes 12615680 | tf_op jit(solution)/shard_map/attend/pallas_call | solution.py:143
  90.5 3.9 %all-to-all-done.3.in_ref = bf16[8,656,128]{2,1,0:T(8,128)(2,1)S(1)} async-done(((bf16[8,656,128]{2,1,0:T(8,128)(2,1)}), bf16[8,656,128]{2,1,0:T(8,128)(2,1)S(1)}, u32[]{:S(2)}, u32[]{:S(2)}) %all-to-all-start.3) | async-done | bytes 1343520 | tf_op jit(solution)/shard_map/all_to_all | solution.py:434
  94.9 3.7 %all-to-all-start.4 = ((bf16[8,1424,128]{2,1,0:T(8,128)(2,1)}), bf16[8,1424,128]{2,1,0:T(8,128)(2,1)S(1)}, u32[]{:S(2)}, u32[]{:S(2)}) async-start(bf16[8,1424,128]{2,1,0:T(8,128)(2,1)} %attend.2), calls=%async_computation.4 | async-start | bytes 5832704 | tf_op jit(solution)/shard_map/all_to_all | solution.py:434
  99.4 31.8 %all-to-all-done.4.in_ref = bf16[8,1424,128]{2,1,0:T(8,128)(2,1)S(1)} async-done(((bf16[8,1424,128]{2,1,0:T(8,128)(2,1)}), bf16[8,1424,128]{2,1,0:T(8,128)(2,1)S(1)}, u32[]{:S(2)}, u32[]{:S(2)}) %all-to-all-start.4) | async-done | bytes 2916384 | tf_op jit(solution)/shard_map/all_to_all | solution.py:434
  131.2 2.8 %merge_late.1 = bf16[8,80,128]{2,1,0:T(8,128)(2,1)} custom-call(bf16[160,512]{1,0:T(8,128)(2,1)S(1)} %get-tuple-element.36.early_ref, f32[8,160]{1,0:T(8,128)S(1)} %get-tuple-element.37.stat_ref, bf16[8,1424,128]{2,1,0:T(8,128)(2,1)S(1)} %all-to-all-done.4.in_ref, bf16[8,2,512,128]{3,2,1,0:T(8,128)(2,1)} %bitcast.35), custom_call_target="tpu_custom_call" | custom-call | tf_op jit(solution)/shard_map/merge_late/pallas_call | solution.py:266
  134.0 3.4 %all-to-all-start.5 = ((bf16[8,80,128]{2,1,0:T(8,128)(2,1)}), bf16[8,80,128]{2,1,0:T(8,128)(2,1)S(1)}, u32[]{:S(2)}, u32[]{:S(2)}) async-start(bf16[8,80,128]{2,1,0:T(8,128)(2,1)} %merge_late.1), calls=%async_computation.5 | async-start | bytes 327680 | tf_op jit(solution)/shard_map/all_to_all | solution.py:434
  137.5 9.3 %all-to-all-done.5.in_ref = bf16[8,80,128]{2,1,0:T(8,128)(2,1)S(1)} async-done(((bf16[8,80,128]{2,1,0:T(8,128)(2,1)}), bf16[8,80,128]{2,1,0:T(8,128)(2,1)S(1)}, u32[]{:S(2)}, u32[]{:S(2)}) %all-to-all-start.5) | async-done | bytes 163872 | tf_op jit(solution)/shard_map/all_to_all | solution.py:434
  146.8 3.3 %project.1 = bf16[64,4,896]{2,1,0:T(4,128)(2,1)} custom-call(s32[1]{0:T(128)} %bitcast.9.place, bf16[8,80,128]{2,1,0:T(8,128)(2,1)S(1)} %all-to-all-done.5.in_ref, bf16[256,7168]{1,0:T(8,128)(2,1)} %far_ref.1), custom_call_target="tpu_custom_call" | custom-call | tf_op jit(solution)/shard_map/project/pallas_call | solution.py:322
  150.1 4.8 %all-to-all-start.6 = ((bf16[64,4,896]{2,1,0:T(4,128)(2,1)}), bf16[64,4,896]{2,1,0:T(4,128)(2,1)S(1)}, u32[]{:S(2)}, u32[]{:S(2)}) async-start(bf16[64,4,896]{2,1,0:T(4,128)(2,1)} %project.1), calls=%async_computation.6 | async-start | bytes 917504 | tf_op jit(solution)/shard_map/all_to_all | solution.py:434
  155.3 14.5 %all-to-all-done.6 = bf16[64,4,896]{2,1,0:T(4,128)(2,1)S(1)} async-done(((bf16[64,4,896]{2,1,0:T(4,128)(2,1)}), bf16[64,4,896]{2,1,0:T(4,128)(2,1)S(1)}, u32[]{:S(2)}, u32[]{:S(2)}) %all-to-all-start.6) | async-done | bytes 458784 | tf_op jit(solution)/shard_map/all_to_all | solution.py:434
  171.0 5.7 %all-to-all-start.7 = ((bf16[64,2,896]{2,1,0:T(2,128)(2,1)}), bf16[64,2,896]{2,1,0:T(2,128)(2,1)S(1)}, u32[]{:S(2)}, u32[]{:S(2)}) async-start(bf16[64,2,896]{2,1,0:T(2,128)(2,1)} %reshape.171), calls=%async_computation.7 | async-start | bytes 458752 | tf_op jit(solution)/shard_map/all_to_all | solution.py:434
  176.9 11.4 %all-to-all-done.7 = bf16[64,2,896]{2,1,0:T(2,128)(2,1)S(1)} async-done(((bf16[64,2,896]{2,1,0:T(2,128)(2,1)}), bf16[64,2,896]{2,1,0:T(2,128)(2,1)S(1)}, u32[]{:S(2)}, u32[]{:S(2)}) %all-to-all-start.7) | async-done | bytes 229408 | tf_op jit(solution)/shard_map/all_to_all | solution.py:434
  188.4 3.0 %experts.1 = bf16[64,2,896]{2,1,0:T(2,128)(2,1)S(1)} custom-call(s32[1]{0:T(128)} %bitcast.11.me, bf16[8,16,896]{2,1,0:T(8,128)(2,1)S(1)} %reshape.172.hid_ref, bf16[8,1,896]{2,1,0:T(2,128)(2,1)S(1)} %reshape.182.gain_ref, bf16[8,8,896]{2,1,0:T(8,128)(2,1)S(1)} %bitcast.30, s32[16,2]{1,0:T(8,128)S(1)} %bitcast.31, bf16[8,896,128]{2,1,0:T(8,128)(2,1)S(1)} %bitcast.29, ...), custom_call_target="tpu_custom_call" | custom-call | tf_op jit(solution)/shard_map/experts/pallas_call | solution.py:389
  191.4 16.0 %all_to_all.46 = bf16[64,2,896]{2,1,0:T(2,128)(2,1)S(1)} all-to-all(bf16[64,2,896]{2,1,0:T(2,128)(2,1)S(1)} %experts.1), channel_id=1, replica_groups=mesh['ctx'=8,'exp'=8,'req'=4] {'ctx','exp'}, dimensions={0} | all-to-all | bytes 458752 | tf_op jit(solution)/shard_map/all_to_all | solution.py:434
  (60 shorter events, 7.8 us)
Async XLA Ops:
  6.5 6.9 %slice-start = ((bf16[16,2,2,576]{3,2,1,0:T(2,128)(2,1)}), bf16[5,2,2,576]{3,2,1,0:T(2,128)(2,1)S(1)}, s32[]{:S(2)}) async-start(bf16[16,2,2,576]{3,2,1,0:T(2,128)(2,1)} %param.14), calls=%async_computation.11 | async-start | bytes 51200 | tf_op jit(solution)/shard_map/slice | solution.py:445
  8.3 14.8 %all-to-all-start = ((bf16[8,44,576]{2,1,0:T(8,128)(2,1)}), bf16[8,44,576]{2,1,0:T(8,128)(2,1)S(1)}, u32[]{:S(2)}, u32[]{:S(2)}) async-start(bf16[8,44,576]{2,1,0:T(8,128)(2,1)} %broadcast_in_dim.20), calls=%async_computation | async-start | bytes 983040 | tf_op jit(solution)/shard_map/all_to_all | solution.py:434
  13.4 64.4 %all-gather.5.cloned.1.call-start = ((), (), s32[]{:S(2)}) async-start(), calls=%async_computation.9 | async-start | bytes 4055040 | tf_op jit(solution)/shard_map/all_gather | solution.py:446
  44.7 4.4 %copy-start.4 = (s32[4,2]{0,1:T(2,128)S(1)}, s32[4,2]{0,1:T(2,128)}, u32[]{:S(2)}) copy-start(s32[4,2]{0,1:T(2,128)} %param.22) | copy-start | bytes 100
  44.7 23.4 %copy-start.2 = (s32[16]{0:T(128)S(1)}, s32[16]{0:T(128)}, u32[]{:S(2)}) copy-start(s32[16]{0:T(128)} %lengths.3) | copy-start | bytes 196
  44.7 23.4 %all-to-all-start.2 = ((bf16[8,160,576]{2,1,0:T(8,128)(2,1)}), bf16[8,160,576]{2,1,0:T(8,128)(2,1)S(1)}, u32[]{:S(2)}, u32[]{:S(2)}) async-start(bf16[8,160,576]{2,1,0:T(8,128)(2,1)} %broadcast_in_dim.23), calls=%async_computation.2 | async-start | bytes 3276800 | tf_op jit(solution)/shard_map/all_to_all | solution.py:434
  74.2 20.3 %all-to-all-start.3 = ((bf16[8,656,128]{2,1,0:T(8,128)(2,1)}), bf16[8,656,128]{2,1,0:T(8,128)(2,1)S(1)}, u32[]{:S(2)}, u32[]{:S(2)}) async-start(bf16[8,656,128]{2,1,0:T(8,128)(2,1)} %attend.3), calls=%async_computation.3 | async-start | bytes 2686976 | tf_op jit(solution)/shard_map/all_to_all | solution.py:434
  77.8 53.4 %all-gather.7.cloned.1.call-start = ((), (), s32[]{:S(2)}) async-start(), calls=%async_computation.10 | async-start | bytes 2359296 | tf_op jit(solution)/shard_map/all_gather | solution.py:457
  94.9 36.3 %all-to-all-start.4 = ((bf16[8,1424,128]{2,1,0:T(8,128)(2,1)}), bf16[8,1424,128]{2,1,0:T(8,128)(2,1)S(1)}, u32[]{:S(2)}, u32[]{:S(2)}) async-start(bf16[8,1424,128]{2,1,0:T(8,128)(2,1)} %attend.2), calls=%async_computation.4 | async-start | bytes 5832704 | tf_op jit(solution)/shard_map/all_to_all | solution.py:434
  134.0 12.7 %all-to-all-start.5 = ((bf16[8,80,128]{2,1,0:T(8,128)(2,1)}), bf16[8,80,128]{2,1,0:T(8,128)(2,1)S(1)}, u32[]{:S(2)}, u32[]{:S(2)}) async-start(bf16[8,80,128]{2,1,0:T(8,128)(2,1)} %merge_late.1), calls=%async_computation.5 | async-start | bytes 327680 | tf_op jit(solution)/shard_map/all_to_all | solution.py:434
  146.8 8.3 %copy-start.3 = (bf16[7168]{0:T(1024)(128)(2,1)S(1)}, bf16[7168]{0:T(1024)(128)(2,1)}, u32[]{:S(2)}) copy-start(bf16[7168]{0:T(1024)(128)(2,1)} %param.20) | copy-start | bytes 43012
  150.0 38.4 %copy-start = (bf16[1,7168,128]{2,1,0:T(8,128)(2,1)S(1)}, bf16[1,7168,128]{2,1,0:T(8,128)(2,1)}, u32[]{:S(2)}) copy-start(bf16[1,7168,128]{2,1,0:T(8,128)(2,1)} %param.23) | copy-start | bytes 5505028
  150.0 38.4 %copy-start.1 = (bf16[7168,8]{0,1:T(8,128)(2,1)S(1)}, bf16[7168,8]{0,1:T(8,128)(2,1)}, u32[]{:S(2)}) copy-start(bf16[7168,8]{0,1:T(8,128)(2,1)} %param.21) | copy-start | bytes 344068
  150.1 19.7 %all-to-all-start.6 = ((bf16[64,4,896]{2,1,0:T(4,128)(2,1)}), bf16[64,4,896]{2,1,0:T(4,128)(2,1)S(1)}, u32[]{:S(2)}, u32[]{:S(2)}) async-start(bf16[64,4,896]{2,1,0:T(4,128)(2,1)} %project.1), calls=%async_computation.6 | async-start | bytes 917504 | tf_op jit(solution)/shard_map/all_to_all | solution.py:434
  171.0 17.3 %all-to-all-start.7 = ((bf16[64,2,896]{2,1,0:T(2,128)(2,1)}), bf16[64,2,896]{2,1,0:T(2,128)(2,1)S(1)}, u32[]{:S(2)}, u32[]{:S(2)}) async-start(bf16[64,2,896]{2,1,0:T(2,128)(2,1)} %reshape.171), calls=%async_computation.7 | async-start | bytes 458752 | tf_op jit(solution)/shard_map/all_to_all | solution.py:434
Sparse Core Ops, SparseCore 0:
  24.6 50.7 all-gather.4
  80.4 38.0 all-gather.6
